TPU v7x, 32 devices: a whole 2x2x4 slice. The times are simulated.
32 devices in a mesh: pole: 2 (over x), row: 16 (over z, y, core).
Axes of the slice: x: 2, y: 2, z: 4, core: 2. Of those that a mesh axis runs over, the one named last changes fastest.
Arguments:
- root_inverse: float32 [4096, 2048], P(('pole', 'row')), parts along dimension 0, may hold values from -6 to 6
- panels: float32 [32, 1024, 512], P(('pole', 'row')), parts along dimension 0, may hold values from -0.1875 to 0.1875
- diag_blocks: float32 [32, 512, 512], P(('pole', 'row')), parts along dimension 0, may hold values from -3 to 3
- structure: int32 [16, 1024], replicated, may hold values from 0 to 2047, as said below
- live: int32 [16], replicated, may hold values from 256 to 1024, as said below
Outputs:
- block_rows: float32 [4096, 16, 512], P(('pole', 'row')), parts along dimension 0
- child_inverse: float32 [32, 512, 512], P(('pole', 'row')), parts along dimension 0
There are 2 independent parts, one for each index of `pole`. A program takes and returns all parts, laid end to end along the dimension named above; an argument that names none is the same for every part. Nothing has to cross between parts.
Inputs may be any that keep to these rules, and one draw needn't show every extreme that they name: `structure`: row j holds live[j] distinct root rows in increasing order, then zeros. `live`: the largest is 1024 in every draw.
All inputs are finite; a program needn't handle non-finite values.
Results may differ from a plain program's by a relative error of at most 0.0003.
Values sent between devices are 32-bit elements; how exact they have to be, the bound alone decides.
No kernel may reach another device: no remote copies, remote signals or barrier semaphores. Data moves between devices by JAX's collectives and lax.ppermute only.
A program may use at most 128 MiB of HBM per device.

v0:
```python
import jax
import jax.numpy as jnp
from jax import lax
from jax.sharding import PartitionSpec as P


def body(root_inverse, panels, diag_blocks, structure, live):
    me = lax.axis_index("row")
    rows_here = root_inverse.shape[0]
    padded = structure.shape[1]
    width = panels.shape[2]
    total_rows = rows_here * lax.axis_size("row")
    mine = lax.dynamic_index_in_dim(structure, me, 0, keepdims=False)
    count = lax.dynamic_index_in_dim(live, me, 0, keepdims=False)
    columns = jnp.take(lax.all_gather(root_inverse, "row", axis=0, tiled=True), mine, axis=1)
    sub = jnp.take(columns, mine, axis=0)
    positions = jnp.arange(padded, dtype=jnp.int32)
    mask = (positions < count).astype(jnp.float32)
    masked = panels[0] * mask[:, None]
    off = -jnp.dot(sub, masked, precision=lax.Precision.HIGHEST) * mask[:, None]
    inner = diag_blocks[0] - jnp.dot(masked.T, off, precision=lax.Precision.HIGHEST)
    spread = jnp.zeros((total_rows, width), jnp.float32).at[mine].add(off)
    block_rows = lax.all_to_all(
        spread.reshape(total_rows, 1, width), "row", split_axis=0, concat_axis=1, tiled=True
    )
    return (block_rows, inner[None])


def solution(mesh):
    placed = (
        P(("pole", "row"), None),
        P(("pole", "row"), None, None),
        P(("pole", "row"), None, None),
        P(),
        P(),
    )
    return jax.shard_map(
        body,
        mesh=mesh,
        in_specs=placed,
        out_specs=(P(("pole", "row"), None, None), P(("pole", "row"), None, None)),
        check_vma=False,
    )
```

profile of v0, /device:TPU:13, one launch (start us, length us, event | category | flops | bytes accessed | tf_op | source)
XLA Modules:
  0.0 321.3 jit_solution(14524612086825479236)
XLA Ops:
  7.2 0.0 all-gather.2.cloned.1.call-start
  7.2 2.5 copy.12
  9.7 0.0 all-gather.2.cloned.1.call-update
  9.8 1.2 dynamic_slice.9
  11.0 0.8 compare_select_fusion
  11.8 0.7 fusion.13
  12.5 127.3 %all-gather.2.cloned.1.call-done = f32[2048,2048]{0,1:T(8,128)} async-done(((f32[128,2048]{0,1:T(8,128)}), f32[2048,2048]{0,1:T(8,128)}) %all-gather.2.cloned.1.call-update) | async-done | bytes 16777232 | tf_op jit(solution)/shard_map/all_gather | solution.py:15
  139.8 14.8 %gather_fusion = f32[1024,2048]{1,0:T(8,128)} fusion(f32[2048,2048]{0,1:T(8,128)} %all-gather.2.cloned.1.call-done, s32[1024]{0:T(1024)S(1)} %broadcast_clamp_fusion), kind=kCustom, calls=%fused_computation | custom fusion | bytes 16781312 | tf_op jit(solution)/shard_map/jit(_take)/gather | solution.py:15
  154.6 7.2 %select_bitcast_fusion = f32[2048,1024]{0,1:T(8,128)} fusion(f32[1024,2048]{1,0:T(8,128)} %gather_fusion, pred[1024]{0:T(1024)(128)(4,1)S(1)} %get-tuple-element.9), kind=kLoop, calls=%fused_computation.3 | loop fusion | flops 2097152 | bytes 16778240 | tf_op jit(solution)/shard_map/jit(_take)/select_n | solution.py:15
  161.8 9.3 %copy.13 = f32[2048,1024]{1,0:T(8,128)} copy(f32[2048,1024]{0,1:T(8,128)} %select_bitcast_fusion) | data formatting | bytes 16777216 | tf_op jit(solution)/shard_map/jit(_take)/select_n | solution.py:15
  171.1 0.0 copy-start
  171.1 9.9 %gather_fusion.1 = f32[1024,1024]{1,0:T(8,128)} fusion(f32[2048,1024]{1,0:T(8,128)} %copy.13, s32[1024]{0:T(1024)S(1)} %broadcast_clamp_fusion), kind=kCustom, calls=%fused_computation.1 | custom fusion | bytes 8392704 | tf_op jit(solution)/shard_map/jit(_take)/gather | solution.py:16
  180.9 0.0 copy-done
  181.0 10.2 %negate_multiply_fusion = f32[1024,512]{1,0:T(8,128)} fusion(f32[1,1024,512]{2,1,0:T(8,128)S(1)} %copy-done, f32[1024,1024]{1,0:T(8,128)} %gather_fusion.1, pred[1024]{0:T(1024)(128)(4,1)S(1)} %get-tuple-element.9, f32[1024]{0:T(1024)S(1)} %get-tuple-element.8), kind=kOutput, calls=%fused_computation.7 | convolution fusion | flops 6445072384 | bytes 8393728 | tf_op jit(solution)/shard_map/dot_general | solution.py:20
  191.2 10.3 %scatter_custom_fusion = f32[2048,512]{1,0:T(8,128)} fusion(s32[1024]{0:T(1024)S(1)} %bitcast.29, f32[1024,512]{1,0:T(8,128)} %negate_multiply_fusion, f32[]{:T(128)} %constant.27.clone.1), kind=kCustom, calls=%fused_computation.9 | custom fusion | flops 524288 | bytes 4194816 | tf_op jit(solution)/shard_map/scatter-add | solution.py:22
  201.4 5.9 %reshape.46 = f32[2048,1,512]{2,1,0:T(1,128)} reshape(f32[2048,512]{1,0:T(8,128)} %scatter_custom_fusion) | data formatting | bytes 8388608 | tf_op jit(solution)/shard_map/reshape | solution.py:24
  207.4 0.0 copy-start.1
  207.4 7.6 %all-to-all-start = ((f32[2048,1,512]{2,1,0:T(1,128)}), f32[2048,1,512]{2,1,0:T(1,128)}, u32[]{:S(2)}, u32[]{:S(2)}) async-start(f32[2048,1,512]{2,1,0:T(1,128)} %reshape.46), calls=%async_computation | async-start | bytes 8388608 | tf_op jit(solution)/shard_map/all_to_all | solution.py:23
  214.9 0.0 copy-done.1
  214.9 6.3 %fusion.10 = f32[1,512,512]{2,1,0:T(8,128)} fusion(f32[1024,512]{1,0:T(8,128)} %negate_multiply_fusion, f32[1,1024,512]{2,1,0:T(8,128)S(1)} %copy-done, f32[1,512,512]{2,1,0:T(8,128)S(1)} %copy-done.1, f32[1024]{0:T(1024)S(1)} %get-tuple-element.8), kind=kOutput, calls=%fused_computation.14 | convolution fusion | flops 3222011904 | bytes 6295552 | tf_op jit(solution)/shard_map/dot_general | solution.py:21
  221.3 86.1 %all-to-all-done = f32[2048,1,512]{2,1,0:T(1,128)} async-done(((f32[2048,1,512]{2,1,0:T(1,128)}), f32[2048,1,512]{2,1,0:T(1,128)}, u32[]{:S(2)}, u32[]{:S(2)}) %all-to-all-start) | async-done | bytes 4194336 | tf_op jit(solution)/shard_map/all_to_all | solution.py:23
  307.4 2.6 copy.15
  310.1 4.4 %copy.14 = f32[128,16,512]{2,1,0:T(8,128)} copy(f32[128,16,512]{2,0,1:T(8,128)S(1)} %bitcast.27) | data formatting | bytes 8388608
  (1 shorter events, 0.0 us)
Async XLA Ops:
  7.2 132.6 %all-gather.2.cloned.1.call-start = ((), (), s32[]{:S(2)}) async-start(), calls=%async_computation.1 | async-start | bytes 17825792 | tf_op jit(solution)/shard_map/all_gather | solution.py:15
  171.1 9.9 %copy-start = (f32[1,1024,512]{2,1,0:T(8,128)S(1)}, f32[1,1024,512]{2,1,0:T(8,128)}, u32[]{:S(2)}) copy-start(f32[1,1024,512]{2,1,0:T(8,128)} %param.6) | copy-start | bytes 6291460
  207.4 7.6 %copy-start.1 = (f32[1,512,512]{2,1,0:T(8,128)S(1)}, f32[1,512,512]{2,1,0:T(8,128)}, u32[]{:S(2)}) copy-start(f32[1,512,512]{2,1,0:T(8,128)} %param.7) | copy-start | bytes 3145732
  207.4 100.0 %all-to-all-start = ((f32[2048,1,512]{2,1,0:T(1,128)}), f32[2048,1,512]{2,1,0:T(1,128)}, u32[]{:S(2)}, u32[]{:S(2)}) async-start(f32[2048,1,512]{2,1,0:T(1,128)} %reshape.46), calls=%async_computation | async-start | bytes 8388608 | tf_op jit(solution)/shard_map/all_to_all | solution.py:23
Sparse Core Ops, SparseCore 0:
  10.7 129.0 all-gather.1
where the time goes:
time: 322 us; the launch traced here: 321 us
  waiting for transfers between devices  213 us (66%)
  local copies, waits for them, and re-layouts  50.7 us (16%)
  other arithmetic  18.9 us (6%)
  matrix products  16.6 us (5%)
  between operations  14.1 us (4%)
  starting transfers between devices  7.6 us (2%)
    all_gather x1, waiting for transfers between devices, body(): lax.all_gather(root_inverse, 'row', axis=0, tiled=True)  127 us
    all_to_all x1, waiting for transfers between devices, body(): lax.all_to_all(spread.reshape(total_rows, 1, width), 'row', split_axis=0,...  86.1 us
    gather x1, local copies, waits for them, and re-layouts, body(): jnp.take(lax.all_gather(root_inverse, 'row', axis=0, tiled=True), mine, a...  14.8 us
    scatter-add x1, other arithmetic, body(): spread = jnp.zeros((total_rows, width), jnp.float32).at[mine].add(off)  10.3 us
    dot_general x1, matrix products, body(): off = -jnp.dot(sub, masked, precision=lax.Precision.HIGHEST) * mask[:, None]  10.2 us
    gather x1, local copies, waits for them, and re-layouts, body(): sub = jnp.take(columns, mine, axis=0)  9.86 us
    unnamed x7, local copies, waits for them, and re-layouts  9.61 us
    select_n x1, local copies, waits for them, and re-layouts, body(): jnp.take(lax.all_gather(root_inverse, 'row', axis=0, tiled=True), mine, a...  9.28 us
  transfers between devices with their start and end apart: 2, of which 2 were waited for; matrix products, arithmetic and copies ran while one was open for 3% of the time, Pallas kernels for 0%

commit v1 on v0

--- a/solution.py
+++ b/solution.py
@@ -1,7 +1,577 @@
+import functools
+
 import jax
 import jax.numpy as jnp
 from jax import lax
+from jax.experimental import pallas as pl
+from jax.experimental.pallas import tpu as pltpu
 from jax.sharding import PartitionSpec as P
+
+F32 = jnp.float32
+BF16 = jnp.bfloat16
+PLANES = 4
+PLANE = 4
+LANES = 128
+SCALE = 16
+VMEM_BYTES = 36 * 1024 * 1024
+LARGE_BYTES = 58 * 1024 * 1024
+
+
+def split(x):
+    hi = x.astype(BF16)
+    return hi, (x - hi.astype(F32)).astype(BF16)
+
+
+def dot(a, b):
+    return jnp.dot(a, b, preferred_element_type=F32)
+
+
+def dot_t(a, b):
+    return lax.dot_general(a, b, (((0,), (0,)), ((), ())), preferred_element_type=F32)
+
+
+class Table:
+    def __init__(self, children, blocks):
+        self.children, self.blocks = children, blocks
+        self.first = 0
+        self.offset = children * blocks
+        self.live = 2 * children * blocks
+        self.me = self.live + children
+        self.over = self.me + 1
+
+
+def window(tab, t, s_ref, child, block, rows, padded):
+    span = min(2 * rows, padded)
+    begin = tab[t.first + child * t.blocks + block]
+    at = pl.multiple_of(jnp.minimum((begin // rows) * rows, padded - span), rows)
+    row_ids = lax.broadcasted_iota(jnp.int32, (rows, span), 0) + block * rows
+    positions = lax.broadcasted_iota(jnp.int32, (rows, span), 1) + at
+    hit = (row_ids == s_ref[child, :, pl.ds(at, span)]) & (positions < tab[t.live + child])
+    return at, span, positions, hit
+
+
+def slots(tab, t, s_ref, child, block, rows, padded):
+    _, _, positions, hit = window(tab, t, s_ref, child, block, rows, padded)
+    shift = tab[t.offset + child * t.blocks + block] - tab[t.first + child * t.blocks + block]
+    return jnp.max(jnp.where(hit, positions + shift, -1), axis=1, keepdims=True)
+
+
+def spread_block(t, tab, s_ref, child, block, rows, panel, hi_ref, lo_ref, to):
+    at, span, _, hit = window(tab, t, s_ref, child, block, rows, s_ref.shape[2])
+    hot = hit.astype(BF16)
+    hi, lo = split(panel[0, pl.ds(at, span), :])
+    hi_ref[0, to, :] = dot(hot, hi).astype(BF16)
+    lo_ref[0, to, :] = dot(hot, lo).astype(BF16)
+
+
+def spread_kernel(t, flips, unroll, tab, s_ref, *refs):
+    panels, (hi_ref, lo_ref) = refs[: len(flips)], refs[len(flips) :]
+    rows = hi_ref.shape[1] // unroll
+    for c, flip in enumerate(flips):
+
+        @pl.when(pl.program_id(0) == c)
+        def _():
+            child = tab[t.me] ^ flip
+            for u in range(unroll):
+                block = pl.program_id(1) * unroll + u
+                to = slice(u * rows, (u + 1) * rows)
+                spread_block(t, tab, s_ref, child, block, rows, panels[c], hi_ref, lo_ref, to)
+
+
+def product_kernel(t, flips, here, there, summed, spreads, deltas, cap, prior, tab, s_ref, *refs):
+    count = len(here)
+    priors, blocks, refs = refs[:prior], refs[prior : prior + count], refs[prior + count :]
+    if spreads:
+        panels, refs = refs[:2], refs[2:]
+    if there:
+        rest_ref, refs = refs[0], refs[1:]
+    hi_ref, lo_ref, out_ref, refs = refs[0], refs[1], refs[2], refs[3:]
+    if summed:
+        kept_ref, sent_ref, refs = refs[0], refs[1], refs[2:]
+    messages, x_ref = refs[:-1], refs[-1]
+    rows = blocks[0].shape[0]
+    m = rows * count
+    padded = s_ref.shape[2]
+    me = tab[t.me]
+    step = pl.program_id(0)
+
+    @pl.when(step == 0)
+    def _():
+        for k in range(count):
+            hi, lo = split(blocks[k][...])
+            x_ref[pl.ds(k * rows, rows), :] = hi
+            x_ref[pl.ds(m + k * rows, rows), :] = lo
+
+    if spreads:
+        for c, flip in enumerate(flips):
+
+            @pl.when(step == c)
+            def _(panel=panels[c], flip=flip):
+                for block in range(t.blocks):
+                    to = slice(block * rows, (block + 1) * rows)
+                    spread_block(t, tab, s_ref, me ^ flip, block, rows, panel, hi_ref, lo_ref, to)
+
+    both = dot(x_ref[...], hi_ref[0])
+    product = both[:m] + both[m:] + dot(x_ref[:m, :], lo_ref[0])
+    out_ref[0] = product
+    child = me ^ jnp.where(step == 0, flips[0], flips[1])
+    slot_ids = lax.broadcasted_iota(jnp.int32, (rows, cap), 1)
+    for n, (message, (k, delta)) in enumerate(zip(messages, deltas)):
+        hot = slots(tab, t, s_ref, child, delta(me, t.blocks), rows, padded) == slot_ids
+        hi, lo = split(product[k * rows : (k + 1) * rows])
+        part = dot_t(hot.astype(BF16), hi) + dot_t(hot.astype(BF16), lo)
+
+        @pl.when(step == 0)
+        def _(n=n, message=message, part=part):
+            message[...] = part + priors[n][...] if prior else part
+
+        @pl.when(step != 0)
+        def _(message=message, part=part):
+            message[...] += part
+
+    if summed:
+        values = jnp.concatenate([product, rest_ref[0]], axis=0) if there else product
+        at = [pl.multiple_of(delta(me, t.blocks) * rows, rows) for delta in here + there]
+        bh = jnp.concatenate([hi_ref[0, pl.ds(k, rows), :] for k in at], axis=0)
+        bl = jnp.concatenate([lo_ref[0, pl.ds(k, rows), :] for k in at], axis=0)
+        hi, lo = split(values)
+        inner = dot_t(bh, hi) + dot_t(bh, lo) + dot_t(bl, hi)
+
+        @pl.when(step == 0)
+        def _():
+            kept_ref[...] = inner
+
+        @pl.when(step != 0)
+        def _():
+            sent_ref[...] = inner
+
+
+def last_kernel(t, cap, tab, s_ref, third_ref, hi_a, lo_a, hi_b, lo_b, out_ref, message, x_ref):
+    rows = third_ref.shape[0]
+    padded = s_ref.shape[2]
+    me = tab[t.me]
+    step = pl.program_id(0)
+
+    @pl.when(step == 0)
+    def _():
+        hi, lo = split(third_ref[...])
+        x_ref[:rows, :] = hi
+        x_ref[rows:, :] = lo
+
+    slot_ids = lax.broadcasted_iota(jnp.int32, (rows, cap), 1)
+    for flip, (hi_ref, lo_ref) in enumerate(((hi_a, lo_a), (hi_a, lo_a), (hi_b, lo_b), (hi_b, lo_b))):
+
+        @pl.when(step == flip)
+        def _(flip=flip, hi_ref=hi_ref, lo_ref=lo_ref):
+            both = dot(x_ref[...], hi_ref[0])
+            product = both[:rows] + both[rows:] + dot(x_ref[:rows, :], lo_ref[0])
+            out_ref[0] = product
+            hot = slots(tab, t, s_ref, me ^ flip, mirror(me, t.blocks), rows, padded) == slot_ids
+            hi, lo = split(product)
+            part = dot_t(hot.astype(BF16), hi) + dot_t(hot.astype(BF16), lo)
+            if flip == 0:
+                message[...] = part
+            else:
+                message[...] += part
+
+
+def finish_kernel(tab, diag_ref, kept_ref, sibling_ref, other_ref, *refs):
+    products, (factors_hi, factors_lo, out_ref) = refs[:4], (refs[4:8], refs[8:12], refs[12])
+    hi, lo = split(jnp.concatenate([g[0] for g in products], axis=0))
+    bh = jnp.concatenate([b[0] for b in factors_hi], axis=0)
+    bl = jnp.concatenate([b[0] for b in factors_lo], axis=0)
+    added = dot_t(bh, hi) + dot_t(bh, lo) + dot_t(bl, hi)
+    out_ref[0] = diag_ref[0] + (kept_ref[...] + sibling_ref[...] + other_ref[...] + added)
+
+
+def own(me, blocks):
+    return me
+
+
+def below(me, blocks):
+    return jnp.maximum(me - PLANE, 0)
+
+
+def above(me, blocks):
+    return jnp.minimum(me + PLANE, blocks - 1)
+
+
+def across(me, blocks):
+    return me ^ (2 * PLANE)
+
+
+def mirror(me, blocks):
+    return me ^ (3 * PLANE)
+
+
+def store(lanes_ref, t, total, width, child, value, late=False):
+    lanes = lanes_ref.shape[1]
+    for k in range(width // lanes):
+        to = pl.ds(k * total + child, total // t.children, stride=t.children)
+        part = value[:, k * lanes : (k + 1) * lanes]
+        lanes_ref[to, :] = lanes_ref[to, :] + part if late else part
+
+
+def unpack(t, tab, s_ref, lanes_ref, total, message, plane, late=False):
+    cap, width = message.shape
+    rows = total // t.children
+    slot_ids = lax.broadcasted_iota(jnp.int32, (rows, cap), 1) + (cap if late else 0)
+    hi, lo = split(message[...])
+    for c in range(PLANE):
+        child = plane * PLANE + c
+        hot = slots(tab, t, s_ref, child, tab[t.me], rows, s_ref.shape[2]) == slot_ids
+        hot = hot.astype(BF16)
+        store(lanes_ref, t, total, width, child, -(dot(hot, hi) + dot(hot, lo)), late)
+
+
+def unpack_kernel(t, tab, s_ref, near_a, near_b, below_ref, above_ref, across_ref, lanes_ref):
+    rows, width = near_a.shape[1:]
+    total = rows * t.children
+    me = tab[t.me]
+    z = me // PLANE
+    for flip in range(PLANE):
+        child = me ^ flip
+        here = slots(tab, t, s_ref, child, me, rows, s_ref.shape[2]) >= 0
+        value = (near_a, near_b)[flip // 2][flip % 2]
+        store(lanes_ref, t, total, width, child, jnp.where(here, -value, 0.0))
+
+    @pl.when(z > 0)
+    def _():
+        unpack(t, tab, s_ref, lanes_ref, total, below_ref, z - 1)
+
+    @pl.when(z < PLANES - 1)
+    def _():
+        unpack(t, tab, s_ref, lanes_ref, total, above_ref, z + 1)
+
+    unpack(t, tab, s_ref, lanes_ref, total, across_ref, z ^ 2)
+
+
+def expand_kernel(t, tab, s_ref, message, lanes_in, late_ref, out_ref, late, lanes_ref, sem):
+    total, width = out_ref.shape
+    lanes = lanes_ref.shape[1]
+    z = tab[t.me] // PLANE
+    at_end = (z == 0) | (z == PLANES - 1)
+    lanes_ref[...] = lanes_in[...]
+
+    @pl.when(at_end)
+    def _():
+        unpack(t, tab, s_ref, lanes_ref, total, message, z ^ 3)
+
+    @pl.when(tab[t.over] != 0)
+    def _():
+        def more(k, carry):
+            there = ((k == 0) & (z > 0)) | ((k == 1) & (z < PLANES - 1)) | (k == 2) | ((k == 3) & at_end)
+
+            @pl.when(there)
+            def _():
+                copy = pltpu.make_async_copy(late_ref.at[k], late, sem)
+                copy.start()
+                copy.wait()
+                plane = jnp.where(k == 0, z - 1, jnp.where(k == 1, z + 1, jnp.where(k == 2, z ^ 2, z ^ 3)))
+                unpack(t, tab, s_ref, lanes_ref, total, late, plane, True)
+
+            return carry
+
+        lax.fori_loop(0, PLANE, more, 0)
+
+    for k in range(width // lanes):
+        out_ref[:, k * lanes : (k + 1) * lanes] = lanes_ref[k * total : (k + 1) * total, :]
+
+
+def late_kernel(t, cap, tab, s_ref, values, message):
+    rows = values.shape[2]
+    to, flip = pl.program_id(0), pl.program_id(1)
+    me = tab[t.me]
+    block = jnp.where(
+        to == 0,
+        below(me, t.blocks),
+        jnp.where(to == 1, above(me, t.blocks), jnp.where(to == 2, across(me, t.blocks), mirror(me, t.blocks))),
+    )
+    slot_ids = lax.broadcasted_iota(jnp.int32, (rows, cap), 1) + cap
+    hot = slots(tab, t, s_ref, me ^ flip, block, rows, s_ref.shape[2]) == slot_ids
+    hi, lo = split(values[0, 0])
+    part = dot_t(hot.astype(BF16), hi) + dot_t(hot.astype(BF16), lo)
+
+    @pl.when(flip == 0)
+    def _():
+        message[0] = part
+
+    @pl.when(flip != 0)
+    def _():
+        message[0] += part
+
+
+def vmem():
+    return pl.BlockSpec(memory_space=pltpu.VMEM)
+
+
+def smem():
+    return pl.BlockSpec(memory_space=pltpu.SMEM)
+
+
+def params(limit=VMEM_BYTES):
+    return pltpu.CompilerParams(vmem_limit_bytes=limit)
+
+
+def cost(flops, bytes_accessed):
+    return pl.CostEstimate(
+        flops=int(flops) // SCALE, bytes_accessed=int(bytes_accessed) // SCALE, transcendentals=0
+    )
+
+
+def after(x, *others):
+    return lax.optimization_barrier((x, *others))[0]
+
+
+def planes_body(cap, table, root_inverse, panels, diag_blocks, structure3):
+    rows, total = root_inverse.shape
+    children = structure3.shape[0]
+    blocks = total // rows
+    width = panels.shape[2]
+    t = Table(children, blocks)
+
+    def permute(x, move):
+        return lax.ppermute(x, "row", [(r, move(r)) for r in range(blocks)])
+
+    def along(x, planes, step):
+        return lax.ppermute(
+            x, "row", [(p * PLANE + b, (p + step) * PLANE + b) for p in planes for b in range(PLANE)]
+        )
+
+    def mirrored(x):
+        ends = (0, PLANES - 1)
+        return lax.ppermute(
+            x, "row", [(p * PLANE + b, (PLANES - 1 - p) * PLANE + b) for p in ends for b in range(PLANE)]
+        )
+
+    def spread(flips, *given):
+        unroll = 4
+        shape = jax.ShapeDtypeStruct((len(flips), total, width), BF16)
+        out = pl.BlockSpec((1, unroll * rows, width), lambda c, i: (c, i, 0))
+        return pl.pallas_call(
+            functools.partial(spread_kernel, t, flips, unroll),
+            grid=(len(flips), blocks // unroll),
+            out_shape=(shape, shape),
+            in_specs=[smem(), vmem()] + [vmem()] * len(given),
+            out_specs=(out, out),
+            compiler_params=params(),
+            cost_estimate=cost(8 * len(flips) * total * rows * 2 * width, 12 * len(flips) * total * width),
+            name="spread",
+        )(table, structure3, *given)
+
+    def product(flips, here, deltas, factors, priors, given, summed=False, there=(), rest=None, panels=()):
+        m = rows * len(given)
+        message = jax.ShapeDtypeStruct((cap, width), F32)
+        square = jax.ShapeDtypeStruct((width, width), F32)
+        factor = jax.ShapeDtypeStruct((2, total, width), BF16)
+        partial_sums = [square, square] if summed else []
+        still = pl.BlockSpec((width, width), lambda c: (0, 0))
+        whole = pl.BlockSpec((1, total, width), lambda c: (c, 0, 0))
+        other_products = [rest] if there else []
+        made = 2 if panels else 0
+        return pl.pallas_call(
+            functools.partial(
+                product_kernel, t, flips, here, there, summed, bool(panels), deltas, cap, len(priors)
+            ),
+            grid=(2,),
+            out_shape=[factor] * made
+            + [jax.ShapeDtypeStruct((2, m, width), F32)]
+            + partial_sums
+            + [message] * len(deltas),
+            in_specs=[smem(), vmem()]
+            + [vmem()] * (len(priors) + len(given) + len(panels))
+            + [pl.BlockSpec((1, rows * len(there), width), lambda c: (c, 0, 0))] * len(other_products)
+            + [whole] * len(factors),
+            out_specs=[whole] * made
+            + [pl.BlockSpec((1, m, width), lambda c: (c, 0, 0))]
+            + [still] * len(partial_sums)
+            + [pl.BlockSpec((cap, width), lambda c: (0, 0))] * len(deltas),
+            scratch_shapes=[pltpu.VMEM((2 * m, total), BF16)],
+            compiler_params=params(),
+            cost_estimate=cost(20 * m * total * width, 4 * len(given) * rows * total + 16 * total * width),
+            name="product",
+        )(table, structure3, *priors, *given, *panels, *other_products, *factors)
+
+    def of_a(c):
+        return jnp.minimum(c, 1)
+
+    def of_b(c):
+        return jnp.maximum(c - 2, 0)
+
+    def final(factors_a, factors_b, third):
+        a = pl.BlockSpec((1, total, width), lambda c: (of_a(c), 0, 0))
+        b = pl.BlockSpec((1, total, width), lambda c: (of_b(c), 0, 0))
+        return pl.pallas_call(
+            functools.partial(last_kernel, t, cap),
+            grid=(PLANE,),
+            out_shape=(
+                jax.ShapeDtypeStruct((PLANE, rows, width), F32),
+                jax.ShapeDtypeStruct((cap, width), F32),
+            ),
+            in_specs=[smem()] + [vmem()] * 2 + [a, a, b, b],
+            out_specs=(
+                pl.BlockSpec((1, rows, width), lambda c: (c, 0, 0)),
+                pl.BlockSpec((cap, width), lambda c: (0, 0)),
+            ),
+            scratch_shapes=[pltpu.VMEM((2 * rows, total), BF16)],
+            compiler_params=params(LARGE_BYTES),
+            cost_estimate=cost(40 * rows * total * width, 32 * total * width),
+            name="last",
+        )(table, structure3, third, *factors_a, *factors_b)
+
+    def finish(kept, sibling, other, last, others, factors):
+        def factor(flip):
+            return pl.BlockSpec(
+                (1, rows, width), lambda i, tab: (0, mirror(tab[t.me] ^ flip, blocks), 0)
+            )
+
+        first_of = pl.BlockSpec((1, width, width), lambda i, tab: (0, 0, 0))
+        pieces = [pl.BlockSpec((1, rows, width), lambda i, tab: (0, 0, 0))] * PLANE
+        return pl.pallas_call(
+            finish_kernel,
+            out_shape=jax.ShapeDtypeStruct((1, width, width), F32),
+            grid_spec=pltpu.PrefetchScalarGridSpec(
+                num_scalar_prefetch=1,
+                grid=(1,),
+                in_specs=[first_of]
+                + [pl.BlockSpec((width, width), lambda i, tab: (0, 0))] * 3
+                + pieces
+                + [factor(flip) for flip in range(PLANE)] * 2,
+                out_specs=first_of,
+            ),
+            compiler_params=params(),
+            cost_estimate=cost(12 * rows * width * width, 40 * rows * width + 20 * width * width),
+            name="finish",
+        )(table, diag_blocks, kept, sibling, other, last, *others, *([factors[0]] * PLANE), *([factors[1]] * PLANE))
+
+    first, second = (0, 1), (2, 3)
+    near_to = ((1, below), (2, above))
+    panel_1 = permute(panels, lambda r: r ^ 1)
+    panel_2 = permute(panels, lambda r: r ^ 2)
+    from_below = along(root_inverse, range(PLANES - 1), 1)
+    from_above = along(root_inverse, range(1, PLANES), -1)
+    factors_a = spread(first, panels, panel_1)
+
+    below_2 = along(after(from_below, *factors_a), range(1, PLANES - 1), 1)
+    above_2 = along(after(from_above, *factors_a), range(1, PLANES - 1), -1)
+    near, far = (own, below, above), (across,)
+    nearby = (root_inverse, from_below, from_above)
+    near_a, down_a, up_a = product(first, near, near_to, factors_a, (), nearby)
+    across_2 = below_2 + above_2
+    middle = range(PLANE, (PLANES - 1) * PLANE)
+    mirror_3 = lax.ppermute(
+        after(across_2, near_a), "row", [(r, r + PLANE if r >= 2 * PLANE else r - PLANE) for r in middle]
+    )
+    panel_3 = permute(after(panel_2, across_2, near_a), lambda r: r ^ 1)
+    far_a, kept_a, sent_a, twice_a = product(
+        first, far, ((0, across),), factors_a, (), (across_2,), True, near, near_a
+    )
+    nearby = (root_inverse, from_below, from_above, across_2)
+    hi_b, lo_b, near_b, kept_b, sent_b, down, up, twice = product(
+        second, near + far, near_to + ((3, across),), (), (down_a, up_a, twice_a), nearby, True,
+        panels=(after(panel_2, kept_a), panel_3),
+    )
+    factors_b = (hi_b, lo_b)
+    got_across = permute(twice, lambda r: r ^ (2 * PLANE))
+    got_below = along(up, range(PLANES - 1), 1)
+    got_above = along(down, range(1, PLANES), -1)
+    sibling_a = permute(after(sent_a, mirror_3), lambda r: r ^ 1)
+    sibling_b = permute(after(sent_b, mirror_3), lambda r: r ^ 1)
+    other = permute(kept_b + sibling_b, lambda r: r ^ 2)
+    last, thrice = final(factors_a, factors_b, after(mirror_3, near_b))
+    got_mirror = mirrored(after(thrice, got_below, got_above, got_across))
+    others = [
+        permute(last[flip : flip + 1], functools.partial(lambda flip, r: r ^ flip, flip))
+        for flip in range(1, PLANE)
+    ]
+    child_inverse = finish(kept_a, sibling_a, other, last, others, factors_a)
+
+    here = pl.BlockSpec((2, rows, width), lambda i: (0, 0, 0))
+    flat = rows * children
+    by_lanes = pl.pallas_call(
+        functools.partial(unpack_kernel, t),
+        grid=(1,),
+        out_shape=jax.ShapeDtypeStruct((flat * (width // LANES), LANES), F32),
+        in_specs=[smem(), vmem(), here, here] + [vmem()] * 3,
+        out_specs=vmem(),
+        compiler_params=params(),
+        cost_estimate=cost(4 * flat * cap * width, 4 * (flat + 5 * cap) * width),
+        name="unpack",
+    )(table, structure3, near_a, near_b, got_below, got_above, got_across)
+
+    def late(near_a, far_a, near_b, last):
+        to_below, to_above, to_across = (
+            jnp.concatenate([near_a[:, k * rows : (k + 1) * rows] if k < 3 else far_a,
+                             near_b[:, k * rows : (k + 1) * rows]])
+            for k in (1, 2, 3)
+        )
+        values = jnp.stack([to_below, to_above, to_across, last])
+        packed = pl.pallas_call(
+            functools.partial(late_kernel, t, cap),
+            grid=(PLANE, PLANE),
+            out_shape=jax.ShapeDtypeStruct((PLANE, cap, width), F32),
+            in_specs=[smem(), vmem(), pl.BlockSpec((1, 1, rows, width), lambda k, c: (k, c, 0, 0))],
+            out_specs=pl.BlockSpec((1, cap, width), lambda k, c: (k, 0, 0)),
+            compiler_params=params(),
+            name="late",
+        )(table, structure3, values)
+        return jnp.stack(
+            [
+                along(packed[1], range(PLANES - 1), 1),
+                along(packed[0], range(1, PLANES), -1),
+                permute(packed[2], lambda r: r ^ (2 * PLANE)),
+                mirrored(packed[3]),
+            ]
+        )
+
+    def none(*unused):
+        return jnp.zeros((PLANE, cap, width), F32)
+
+    more = lax.cond(table[t.over] != 0, late, none, after(near_a, got_mirror, child_inverse, by_lanes), far_a, near_b, last)
+    block_rows = pl.pallas_call(
+        functools.partial(expand_kernel, t),
+        out_shape=jax.ShapeDtypeStruct((flat, width), F32),
+        in_specs=[smem()] + [vmem()] * 3 + [pl.BlockSpec(memory_space=pl.ANY)],
+        out_specs=vmem(),
+        scratch_shapes=[
+            pltpu.VMEM((cap, width), F32),
+            pltpu.VMEM((flat * (width // LANES), LANES), F32),
+            pltpu.SemaphoreType.DMA,
+        ],
+        compiler_params=params(),
+        cost_estimate=cost(flat * cap * width, 8 * flat * width),
+        name="expand",
+    )(table, structure3, got_mirror, after(by_lanes, child_inverse), more)
+    return block_rows.reshape(rows, children, width), child_inverse
+
+
+def planes(root_inverse, panels, diag_blocks, structure, live):
+    rows, total = root_inverse.shape
+    children, padded = structure.shape
+    blocks = total // rows
+    positions = jnp.arange(padded, dtype=jnp.int32)
+    block_of = jnp.where(positions[None, :] < live[:, None], structure // rows, blocks)
+    edges = jnp.arange(blocks + 1, dtype=jnp.int32)
+    first = jnp.sum((block_of[:, None, :] < edges[None, :, None]).astype(jnp.int32), axis=2)
+    counts = (first[:, 1:] - first[:, :-1]).reshape(PLANES, PLANE, blocks)
+    offsets = [jnp.zeros_like(counts[:, 0])]
+    for c in range(PLANE):
+        offsets.append(offsets[-1] + counts[:, c])
+    largest = jnp.max(offsets[-1])
+    offset = jnp.stack(offsets[:-1], axis=1).reshape(children, blocks)
+    cap = 2 * rows
+    table = jnp.concatenate(
+        [
+            first[:, :-1].reshape(-1),
+            offset.reshape(-1),
+            live,
+            lax.axis_index("row").astype(jnp.int32)[None],
+            (largest > cap).astype(jnp.int32)[None],
+        ]
+    )
+    return planes_body(
+        cap, table, root_inverse, panels, diag_blocks, structure.reshape(children, 1, padded)
+    )
 
 
 def body(root_inverse, panels, diag_blocks, structure, live):
@@ -35,7 +605,7 @@
         P(),
     )
     return jax.shard_map(
-        body,
+        planes if mesh.shape["row"] == PLANES * PLANE else body,
         mesh=mesh,
         in_specs=placed,
         out_specs=(P(("pole", "row"), None, None), P(("pole", "row"), None, None)),

time: 322 us -> 170 us (0.53)
  the two profiles are of different devices: /device:TPU:13 before, /device:TPU:1 now
where the time goes in v1:
time: 170 us; the launch traced here: 169 us
  Pallas kernels  66.3 us (39%)
  waiting for transfers between devices  51.6 us (30%)
  starting transfers between devices  32 us (19%)
  local copies, waits for them, and re-layouts  14.4 us (8%)
  other arithmetic  3.34 us (2%)
  between operations  1.77 us (1%)
    pallas_call x3, Pallas kernels, product(): pl.pallas_call(functools.partial(product_kernel, t, flips, here, there, s...  35.1 us
    ppermute x10, waiting for transfers between devices, permute(): return lax.ppermute(x, 'row', [(r, move(r)) for r in range(blocks)])  29.4 us
    ppermute x6, waiting for transfers between devices, along(): lax.ppermute(x, 'row', [(p * PLANE + b, (p + step) * PLANE + b) for p in...  22.2 us
    ppermute x6, starting transfers between devices, along(): lax.ppermute(x, 'row', [(p * PLANE + b, (p + step) * PLANE + b) for p in...  15.9 us
    ppermute x10, starting transfers between devices, permute(): return lax.ppermute(x, 'row', [(r, move(r)) for r in range(blocks)])  12.7 us
    pallas_call x1, Pallas kernels, final(): pl.pallas_call(functools.partial(last_kernel, t, cap), grid=(PLANE,), out...  11.6 us
    unnamed x40, local copies, waits for them, and re-layouts  10.1 us
    pallas_call x1, Pallas kernels, spread(): pl.pallas_call(functools.partial(spread_kernel, t, flips, unroll), grid=(...  6.61 us
  transfers between devices with their start and end apart: 18, of which 5 were waited for; matrix products, arithmetic and copies ran while one was open for 4% of the time, Pallas kernels for 36%

profile of v1, /device:TPU:1, one launch (start us, length us, event | category | flops | bytes accessed | tf_op | source)
XLA Modules:
  0.0 169.4 jit_solution(4891560123072615210)
XLA Ops:
  0.6 0.1 collective-permute-start.5
  0.8 1.3 collective-permute-start.7
  2.0 6.3 %collective-permute-start.4 = (f32[128,2048]{1,0:T(8,128)}, f32[128,2048]{1,0:T(8,128)}, u32[]{:S(2)}, u32[]{:S(2)}) collective-permute-start(f32[128,2048]{1,0:T(8,128)} %refs_3_.1), channel_id=1, source_target_pairs={{0,4},{1,5},{2,6},{3,7},{4,8},{5,9},{6,10},{7,11},{8,12},{9,13},{1... | collective-permute-start | bytes 3145736 | tf_op jit(solution)/shard_map/ppermute | solution.py:337
  8.3 1.4 collective-permute-start.10
  9.7 0.9 reshape.23.s_ref
  10.6 0.9 fusion.1
  11.5 0.4 convert_reduce_fusion
  12.1 0.1 reshape_reshape.3
  12.2 0.6 reduce_max.9
  13.6 0.7 concatenate.12.tab
  14.4 1.7 copy-done.8
  16.0 6.6 %spread.1 = (bf16[2,2048,512]{2,1,0:T(8,128)(2,1)S(1)}, bf16[2,2048,512]{2,1,0:T(8,128)(2,1)S(1)}) custom-call(s32[530]{0:T(1024)S(1)} %concatenate.12.tab, s32[16,1,1024]{2,1,0:T(1,128)S(1)} %reshape.23.s_ref, f32[1,1024,512]{2,1,0:T(8,128)S(1)} %copy-done.8, f32[1,1024,512]{2,1,0:T(8,128)} %collective-permute-done.5.refs_1_), custom_call_target="tpu_custom_call" | custom-call | flops 268435456 | bytes 1572864 | tf_op jit(solution)/shard_map/spread/pallas_call | solution.py:351
  22.7 6.5 %collective-permute-done.7.refs_2_.refs_5_ = f32[128,2048]{1,0:T(8,128)S(1)} collective-permute-done((f32[128,2048]{1,0:T(8,128)}, f32[128,2048]{1,0:T(8,128)S(1)}, u32[]{:S(2)}, u32[]{:S(2)}) %collective-permute-start.7) | collective-permute-done | bytes 1048608 | tf_op jit(solution)/shard_map/ppermute | solution.py:337
  29.2 1.3 collective-permute-start.8
  30.5 0.7 collective-permute-start.6
  31.3 8.5 %product.3 = (f32[2,384,512]{2,1,0:T(8,128)S(1)}, f32[256,512]{1,0:T(8,128)S(1)}, f32[256,512]{1,0:T(8,128)S(1)}) custom-call(s32[530]{0:T(1024)S(1)} %concatenate.12.tab, s32[16,1,1024]{2,1,0:T(1,128)S(1)} %reshape.23.s_ref, f32[128,2048]{1,0:T(8,128)S(1)} %copy-done.7, f32[128,2048]{1,0:T(8,128)} %collective-permute-done.4.refs_1_.refs_4_, ...), custom_call_target="tpu_custom_call" | custom-call | flops 503316480 | bytes 1245184 | tf_op jit(solution)/shard_map/product/pallas_call | solution.py:372
  39.8 15.7 %collective-permute-done.8 = f32[128,2048]{1,0:T(8,128)S(1)} collective-permute-done((f32[128,2048]{1,0:T(8,128)S(1)}, f32[128,2048]{1,0:T(8,128)S(1)}, u32[]{:S(2)}, u32[]{:S(2)}) %collective-permute-start.8) | collective-permute-done | bytes 1048608 | tf_op jit(solution)/shard_map/ppermute | solution.py:337
  55.4 0.1 add.25.refs_0_.refs_6_
  55.6 1.3 collective-permute-start.11
  56.9 1.5 collective-permute-start.9
  58.4 6.6 %product.4 = (f32[2,128,512]{2,1,0:T(8,128)}, f32[512,512]{1,0:T(8,128)S(1)}, f32[512,512]{1,0:T(8,128)}, f32[256,512]{1,0:T(8,128)S(1)}) custom-call(s32[530]{0:T(1024)S(1)} %concatenate.12.tab, s32[16,1,1024]{2,1,0:T(1,128)S(1)} %reshape.23.s_ref, f32[128,2048]{1,0:T(8,128)S(1)} %add.25.refs_0_.refs_6_, ...), custom_call_target="tpu_custom_call" | custom-call | flops 167772160 | bytes 1114112 | tf_op jit(solution)/shard_map/product/pallas_call | solution.py:372
  64.9 1.0 copy-done.10
  66.0 20.1 %product.5 = (bf16[2,2048,512]{2,1,0:T(8,128)(2,1)S(1)}, bf16[2,2048,512]{2,1,0:T(8,128)(2,1)}, f32[2,512,512]{2,1,0:T(8,128)}, f32[512,512]{1,0:T(8,128)S(1)}, ...) custom-call(s32[530]{0:T(1024)S(1)} %concatenate.12.tab, ...), custom_call_target="tpu_custom_call" | custom-call | flops 671088640 | bytes 1310720 | tf_op jit(solution)/shard_map/product/pallas_call | solution.py:372
  86.0 2.1 %copy-done.6 = bf16[2,2048,512]{2,1,0:T(8,128)(2,1)} copy-done((bf16[2,2048,512]{2,1,0:T(8,128)(2,1)}, bf16[2,2048,512]{2,1,0:T(8,128)(2,1)S(1)}, u32[]{:S(2)}) %copy-start.6) | copy-done | bytes 4194328
  88.1 0.5 collective-permute-start.16
  88.6 2.9 %collective-permute-done.17 = f32[512,512]{1,0:T(8,128)S(1)} collective-permute-done((f32[512,512]{1,0:T(8,128)S(1)}, f32[512,512]{1,0:T(8,128)S(1)}, u32[]{:S(2)}, u32[]{:S(2)}) %collective-permute-start.17) | collective-permute-done | bytes 1048608 | tf_op jit(solution)/shard_map/ppermute | solution.py:334
  91.6 1.2 add.26
  92.7 1.1 collective-permute-start.18
  93.9 4.9 %collective-permute-start.12 = (f32[256,512]{1,0:T(8,128)S(1)}, f32[256,512]{1,0:T(8,128)S(1)}, u32[]{:S(2)}, u32[]{:S(2)}) collective-permute-start(f32[256,512]{1,0:T(8,128)S(1)} %get-tuple-element.70), channel_id=1, source_target_pairs={{0,4},{1,5},{2,6},{3,7},{4,8},{5,9},{6,10},{7,11},{8,12},{9,13},{1... | collective-permute-start | bytes 1572872 | tf_op jit(solution)/shard_map/ppermute | solution.py:337
  98.7 1.5 collective-permute-start.13
  100.3 4.7 %collective-permute-start.14 = (f32[256,512]{1,0:T(8,128)S(1)}, f32[256,512]{1,0:T(8,128)S(1)}, u32[]{:S(2)}, u32[]{:S(2)}) collective-permute-start(f32[256,512]{1,0:T(8,128)S(1)} %get-tuple-element.72), channel_id=1, source_target_pairs={{0,8},{1,9},{2,10},{3,11},{4,12},{5,13},{6,14},{7,15},{8,0},{9,1},... | collective-permute-start | bytes 1572872 | tf_op jit(solution)/shard_map/ppermute | solution.py:334
  105.0 11.6 %last.1 = (f32[4,128,512]{2,1,0:T(8,128)}, f32[256,512]{1,0:T(8,128)}) custom-call(s32[530]{0:T(1024)S(1)} %concatenate.12.tab, s32[16,1,1024]{2,1,0:T(1,128)S(1)} %reshape.23.s_ref, f32[128,2048]{1,0:T(8,128)} %copy-done.20, bf16[2,2048,512]{2,1,0:T(8,128)(2,1)} %copy-done, bf16[2,2048,512]{2,1,0:T(8,128)(2,1)} %copy-done.2, ...), custom_call_target="tpu_custom_call" | custom-call | flops 335544320 | bytes 2097152 | tf_op jit(solution)/shard_map/last/pallas_call | solution.py:404
  116.6 21.6 %collective-permute-done.14.across_ref = f32[256,512]{1,0:T(8,128)S(1)} collective-permute-done((f32[256,512]{1,0:T(8,128)S(1)}, f32[256,512]{1,0:T(8,128)S(1)}, u32[]{:S(2)}, u32[]{:S(2)}) %collective-permute-start.14) | collective-permute-done | bytes 524320 | tf_op jit(solution)/shard_map/ppermute | solution.py:334
  138.2 1.9 %collective-permute-start.15 = (f32[256,512]{1,0:T(8,128)}, f32[256,512]{1,0:T(8,128)}, u32[]{:S(2)}, u32[]{:S(2)}) collective-permute-start(f32[256,512]{1,0:T(8,128)} %get-tuple-element.73), channel_id=1, source_target_pairs={{0,12},{1,13},{2,14},{3,15},{12,0},{13,1},{14,2},{15,3},{16,28},{1... | collective-permute-start | bytes 1572872 | tf_op jit(solution)/shard_map/ppermute | solution.py:343
  140.2 2.1 %fusion.5 = (f32[1,128,512]{2,1,0:T(8,128)}, f32[1,128,512]{2,1,0:T(8,128)}, f32[1,128,512]{2,1,0:T(8,128)}) fusion(f32[4,128,512]{2,1,0:T(8,128)} %get-tuple-element.79.refs_0_), kind=kLoop, calls=%fused_computation.27 | loop fusion | bytes 1572864 | tf_op jit(solution)/shard_map/slice | solution.py:484
  142.3 1.8 %collective-permute-start.19 = (f32[1,128,512]{2,1,0:T(8,128)}, f32[1,128,512]{2,1,0:T(8,128)S(1)}, u32[]{:S(2)}, u32[]{:S(2)}) collective-permute-start(f32[1,128,512]{2,1,0:T(8,128)} %get-tuple-element.99), channel_id=1, source_target_pairs={{0,1},{1,0},{2,3},{3,2},{4,5},{5,4},{6,7},{7,6},{8,9},{9,8},{10,11... | collective-permute-start | bytes 786440 | tf_op jit(solution)/shard_map/ppermute | solution.py:334
  144.1 0.3 collective-permute-start.20
  144.4 1.4 collective-permute-start.21
  145.8 1.0 copy-done.13
  146.8 1.0 copy-done.15
  147.9 1.0 copy-done.17
  148.9 4.3 %unpack.1.lanes_in = f32[8192,128]{1,0:T(8,128)S(1)} custom-call(s32[530]{0:T(1024)S(1)} %concatenate.12.tab, s32[16,1,1024]{2,1,0:T(1,128)S(1)} %reshape.23.s_ref, f32[2,384,512]{2,1,0:T(8,128)} %copy-done.18, f32[2,512,512]{2,1,0:T(8,128)} %get-tuple-element.65.near_b, f32[256,512]{1,0:T(8,128)S(1)} %copy-done.13, f32[256,512]{1,0:T(8,128)S(1)} %copy-done.15, ...), custom_call_target="tpu_custom_call" | custom-call | flops 67108864 | bytes 425984 | tf_op jit(solution)/shard_map/unpack/pallas_call | solution.py:491
  153.2 4.8 %collective-permute-done.21.refs_3_ = f32[1,128,512]{2,1,0:T(8,128)} collective-permute-done((f32[1,128,512]{2,1,0:T(8,128)}, f32[1,128,512]{2,1,0:T(8,128)}, u32[]{:S(2)}, u32[]{:S(2)}) %collective-permute-start.21) | collective-permute-done | bytes 262176 | tf_op jit(solution)/shard_map/ppermute | solution.py:334
  158.1 3.7 %finish.1 = f32[1,512,512]{2,1,0:T(8,128)} custom-call(s32[530]{0:T(1024)S(1)} %concatenate.12.tab, f32[1,512,512]{2,1,0:T(8,128)S(1)} %copy-done.9, f32[512,512]{1,0:T(8,128)S(1)} %copy-done.11, f32[512,512]{1,0:T(8,128)S(1)} %collective-permute-done.16.sibling_ref, f32[512,512]{1,0:T(8,128)S(1)} %collective-permute-done.18.other_ref, ...), custom_call_target="tpu_custom_call" | custom-call | flops 25165824 | bytes 491520 | tf_op jit(solution)/shard_map/finish/pallas_call | solution.py:430
  161.8 0.3 conditional.1
  161.8 0.2 broadcast.10
  162.1 2.2 %copy-done.5 = f32[8192,128]{1,0:T(8,128)S(1)} copy-done((f32[8192,128]{1,0:T(8,128)S(1)}, f32[8192,128]{1,0:T(8,128)}, u32[]{:S(2)}) %copy-start.5) | copy-done | bytes 4194328
  164.2 5.0 %expand.1 = f32[2048,512]{1,0:T(8,128)} custom-call(s32[530]{0:T(1024)S(1)} %concatenate.12.tab, s32[16,1,1024]{2,1,0:T(1,128)S(1)} %reshape.23.s_ref, f32[256,512]{1,0:T(8,128)} %collective-permute-done.15.message, f32[8192,128]{1,0:T(8,128)S(1)} %copy-done.5, f32[4,256,512]{2,1,0:T(8,128)S(1)} %get-tuple-element.103.late_ref), custom_call_target="tpu_custom_call" | custom-call | flops 16777216 | bytes 524288 | tf_op jit(solution)/shard_map/expand/pallas_call | solution.py:531
  (54 shorter events, 0.4 us)
Async XLA Ops:
  0.6 13.7 %collective-permute-start.5 = (f32[1,1024,512]{2,1,0:T(8,128)}, f32[1,1024,512]{2,1,0:T(8,128)}, u32[]{:S(2)}, u32[]{:S(2)}) collective-permute-start(f32[1,1024,512]{2,1,0:T(8,128)} %refs_0_.2), channel_id=1, source_target_pairs={{0,1},{1,0},{2,3},{3,2},{4,5},{5,4},{6,7},{7,6},{8,9},{9,8},{10,11... | collective-permute-start | bytes 6291464 | tf_op jit(solution)/shard_map/ppermute | solution.py:334
  0.8 28.5 %collective-permute-start.7 = (f32[128,2048]{1,0:T(8,128)}, f32[128,2048]{1,0:T(8,128)S(1)}, u32[]{:S(2)}, u32[]{:S(2)}) collective-permute-start(f32[128,2048]{1,0:T(8,128)} %refs_3_.1), channel_id=1, source_target_pairs={{4,0},{5,1},{6,2},{7,3},{8,4},{9,5},{10,6},{11,7},{12,8},{13,9},{1... | collective-permute-start | bytes 3145736 | tf_op jit(solution)/shard_map/ppermute | solution.py:337
  2.0 28.5 %collective-permute-start.4 = (f32[128,2048]{1,0:T(8,128)}, f32[128,2048]{1,0:T(8,128)}, u32[]{:S(2)}, u32[]{:S(2)}) collective-permute-start(f32[128,2048]{1,0:T(8,128)} %refs_3_.1), channel_id=1, source_target_pairs={{0,4},{1,5},{2,6},{3,7},{4,8},{5,9},{6,10},{7,11},{8,12},{9,13},{1... | collective-permute-start | bytes 3145736 | tf_op jit(solution)/shard_map/ppermute | solution.py:337
  8.3 47.3 %collective-permute-start.10 = (f32[1,1024,512]{2,1,0:T(8,128)}, f32[1,1024,512]{2,1,0:T(8,128)}, u32[]{:S(2)}, u32[]{:S(2)}) collective-permute-start(f32[1,1024,512]{2,1,0:T(8,128)} %refs_0_.2), channel_id=1, source_target_pairs={{0,2},{1,3},{2,0},{3,1},{4,6},{5,7},{6,4},{7,5},{8,10},{9,11},{10,... | collective-permute-start | bytes 6291464 | tf_op jit(solution)/shard_map/ppermute | solution.py:334
  14.3 16.9 %copy-start.7 = (f32[128,2048]{1,0:T(8,128)S(1)}, f32[128,2048]{1,0:T(8,128)}, u32[]{:S(2)}) copy-start(f32[128,2048]{1,0:T(8,128)} %refs_3_.1) | copy-start | bytes 3145732
  14.4 1.7 copy-start.8
  22.7 35.7 %copy-start = (bf16[2,2048,512]{2,1,0:T(8,128)(2,1)}, bf16[2,2048,512]{2,1,0:T(8,128)(2,1)S(1)}, u32[]{:S(2)}) copy-start(bf16[2,2048,512]{2,1,0:T(8,128)(2,1)S(1)} %get-tuple-element.53.refs_3_.refs_2_.hi_a.refs_4_.refs_5_.refs_6_.refs_7_) | copy-start | bytes 12582916
  22.7 35.7 %copy-start.2 = (bf16[2,2048,512]{2,1,0:T(8,128)(2,1)}, bf16[2,2048,512]{2,1,0:T(8,128)(2,1)S(1)}, u32[]{:S(2)}) copy-start(bf16[2,2048,512]{2,1,0:T(8,128)(2,1)S(1)} %get-tuple-element.54.refs_4_.refs_3_.lo_a.refs_8_.refs_9_.refs_10_.refs_11_) | copy-start | bytes 12582916
  29.2 26.2 %collective-permute-start.8 = (f32[128,2048]{1,0:T(8,128)S(1)}, f32[128,2048]{1,0:T(8,128)S(1)}, u32[]{:S(2)}, u32[]{:S(2)}) collective-permute-start(f32[128,2048]{1,0:T(8,128)S(1)} %collective-permute-done.7.refs_2_.refs_5_), channel_id=1, source_target_pairs={{4,0},{5,1},{6,2},{7,3},{8,4},{9,5},{10,6},{11,7},{20,16},{21,17},... | collective-permute-start | bytes 3145736 | tf_op jit(solution)/shard_map/ppermute | solution.py:337
  30.5 24.9 %collective-permute-start.6 = (f32[128,2048]{1,0:T(8,128)}, f32[128,2048]{1,0:T(8,128)S(1)}, u32[]{:S(2)}, u32[]{:S(2)}) collective-permute-start(f32[128,2048]{1,0:T(8,128)} %collective-permute-done.4.refs_1_.refs_4_), channel_id=1, source_target_pairs={{4,8},{5,9},{6,10},{7,11},{8,12},{9,13},{10,14},{11,15},{20,24},{2... | collective-permute-start | bytes 3145736 | tf_op jit(solution)/shard_map/ppermute | solution.py:337
  39.7 25.2 %copy-start.18 = (f32[2,384,512]{2,1,0:T(8,128)}, f32[2,384,512]{2,1,0:T(8,128)S(1)}, u32[]{:S(2)}) copy-start(f32[2,384,512]{2,1,0:T(8,128)S(1)} %get-tuple-element.81.refs_1_.near_a) | copy-start | bytes 4718596
  55.6 10.4 %collective-permute-start.11 = (f32[1,1024,512]{2,1,0:T(8,128)}, f32[1,1024,512]{2,1,0:T(8,128)S(1)}, u32[]{:S(2)}, u32[]{:S(2)}) collective-permute-start(f32[1,1024,512]{2,1,0:T(8,128)} %collective-permute-done.10.refs_7_), channel_id=1, source_target_pairs={{0,1},{1,0},{2,3},{3,2},{4,5},{5,4},{6,7},{7,6},{8,9},{9,8},{10,11... | collective-permute-start | bytes 6291464 | tf_op jit(solution)/shard_map/ppermute | solution.py:334
  56.9 31.2 %collective-permute-start.9 = (f32[128,2048]{1,0:T(8,128)S(1)}, f32[128,2048]{1,0:T(8,128)S(1)}, u32[]{:S(2)}, u32[]{:S(2)}) collective-permute-start(f32[128,2048]{1,0:T(8,128)S(1)} %add.25.refs_0_.refs_6_), channel_id=1, source_target_pairs={{4,0},{5,1},{6,2},{7,3},{8,12},{9,13},{10,14},{11,15},{20,16},{21,... | collective-permute-start | bytes 3145736 | tf_op jit(solution)/shard_map/ppermute | solution.py:462
  64.9 1.0 copy-start.10
  86.0 2.1 %copy-start.6 = (bf16[2,2048,512]{2,1,0:T(8,128)(2,1)}, bf16[2,2048,512]{2,1,0:T(8,128)(2,1)S(1)}, u32[]{:S(2)}) copy-start(bf16[2,2048,512]{2,1,0:T(8,128)(2,1)S(1)} %get-tuple-element.67.hi_b) | copy-start | bytes 12582916
  88.1 16.9 %copy-start.20 = (f32[128,2048]{1,0:T(8,128)}, f32[128,2048]{1,0:T(8,128)S(1)}, u32[]{:S(2)}) copy-start(f32[128,2048]{1,0:T(8,128)S(1)} %collective-permute-done.9.third_ref) | copy-start | bytes 3145732
  88.1 3.5 %collective-permute-start.17 = (f32[512,512]{1,0:T(8,128)S(1)}, f32[512,512]{1,0:T(8,128)S(1)}, u32[]{:S(2)}, u32[]{:S(2)}) collective-permute-start(f32[512,512]{1,0:T(8,128)S(1)} %get-tuple-element.78), channel_id=1, source_target_pairs={{0,1},{1,0},{2,3},{3,2},{4,5},{5,4},{6,7},{7,6},{8,9},{9,8},{10,11... | collective-permute-start | bytes 3145736 | tf_op jit(solution)/shard_map/ppermute | solution.py:334
  88.1 56.2 %collective-permute-start.16 = (f32[512,512]{1,0:T(8,128)}, f32[512,512]{1,0:T(8,128)S(1)}, u32[]{:S(2)}, u32[]{:S(2)}) collective-permute-start(f32[512,512]{1,0:T(8,128)} %get-tuple-element.75), channel_id=1, source_target_pairs={{0,1},{1,0},{2,3},{3,2},{4,5},{5,4},{6,7},{7,6},{8,9},{9,8},{10,11... | collective-permute-start | bytes 3145736 | tf_op jit(solution)/shard_map/ppermute | solution.py:334
  92.7 65.3 %collective-permute-start.18 = (f32[512,512]{1,0:T(8,128)}, f32[512,512]{1,0:T(8,128)S(1)}, u32[]{:S(2)}, u32[]{:S(2)}) collective-permute-start(f32[512,512]{1,0:T(8,128)} %add.26), channel_id=1, source_target_pairs={{0,2},{1,3},{2,0},{3,1},{4,6},{5,7},{6,4},{7,5},{8,10},{9,11},{10,... | collective-permute-start | bytes 3145736 | tf_op jit(solution)/shard_map/ppermute | solution.py:334
  93.9 22.7 %collective-permute-start.12 = (f32[256,512]{1,0:T(8,128)S(1)}, f32[256,512]{1,0:T(8,128)S(1)}, u32[]{:S(2)}, u32[]{:S(2)}) collective-permute-start(f32[256,512]{1,0:T(8,128)S(1)} %get-tuple-element.70), channel_id=1, source_target_pairs={{0,4},{1,5},{2,6},{3,7},{4,8},{5,9},{6,10},{7,11},{8,12},{9,13},{1... | collective-permute-start | bytes 1572872 | tf_op jit(solution)/shard_map/ppermute | solution.py:337
  98.7 17.9 %collective-permute-start.13 = (f32[256,512]{1,0:T(8,128)S(1)}, f32[256,512]{1,0:T(8,128)S(1)}, u32[]{:S(2)}, u32[]{:S(2)}) collective-permute-start(f32[256,512]{1,0:T(8,128)S(1)} %get-tuple-element.71), channel_id=1, source_target_pairs={{4,0},{5,1},{6,2},{7,3},{8,4},{9,5},{10,6},{11,7},{12,8},{13,9},{1... | collective-permute-start | bytes 1572872 | tf_op jit(solution)/shard_map/ppermute | solution.py:337
  100.3 38.0 %collective-permute-start.14 = (f32[256,512]{1,0:T(8,128)S(1)}, f32[256,512]{1,0:T(8,128)S(1)}, u32[]{:S(2)}, u32[]{:S(2)}) collective-permute-start(f32[256,512]{1,0:T(8,128)S(1)} %get-tuple-element.72), channel_id=1, source_target_pairs={{0,8},{1,9},{2,10},{3,11},{4,12},{5,13},{6,14},{7,15},{8,0},{9,1},... | collective-permute-start | bytes 1572872 | tf_op jit(solution)/shard_map/ppermute | solution.py:334
  116.6 27.8 %copy-start.12 = (f32[256,512]{1,0:T(8,128)}, f32[256,512]{1,0:T(8,128)S(1)}, u32[]{:S(2)}) copy-start(f32[256,512]{1,0:T(8,128)S(1)} %collective-permute-done.12.below_ref) | copy-start | bytes 1572868
  116.6 27.7 %copy-start.14 = (f32[256,512]{1,0:T(8,128)}, f32[256,512]{1,0:T(8,128)S(1)}, u32[]{:S(2)}) copy-start(f32[256,512]{1,0:T(8,128)S(1)} %collective-permute-done.13.above_ref) | copy-start | bytes 1572868
  138.2 6.1 %copy-start.16 = (f32[256,512]{1,0:T(8,128)}, f32[256,512]{1,0:T(8,128)S(1)}, u32[]{:S(2)}) copy-start(f32[256,512]{1,0:T(8,128)S(1)} %collective-permute-done.14.across_ref) | copy-start | bytes 1572868
  138.2 23.5 %collective-permute-start.15 = (f32[256,512]{1,0:T(8,128)}, f32[256,512]{1,0:T(8,128)}, u32[]{:S(2)}, u32[]{:S(2)}) collective-permute-start(f32[256,512]{1,0:T(8,128)} %get-tuple-element.73), channel_id=1, source_target_pairs={{0,12},{1,13},{2,14},{3,15},{12,0},{13,1},{14,2},{15,3},{16,28},{1... | collective-permute-start | bytes 1572872 | tf_op jit(solution)/shard_map/ppermute | solution.py:343
  140.2 17.9 %copy-start.11 = (f32[512,512]{1,0:T(8,128)S(1)}, f32[512,512]{1,0:T(8,128)}, u32[]{:S(2)}) copy-start(f32[512,512]{1,0:T(8,128)} %copy-done.10) | copy-start | bytes 3145732
  142.3 10.9 %collective-permute-start.19 = (f32[1,128,512]{2,1,0:T(8,128)}, f32[1,128,512]{2,1,0:T(8,128)S(1)}, u32[]{:S(2)}, u32[]{:S(2)}) collective-permute-start(f32[1,128,512]{2,1,0:T(8,128)} %get-tuple-element.99), channel_id=1, source_target_pairs={{0,1},{1,0},{2,3},{3,2},{4,5},{5,4},{6,7},{7,6},{8,9},{9,8},{10,11... | collective-permute-start | bytes 786440 | tf_op jit(solution)/shard_map/ppermute | solution.py:334
  144.1 9.1 %collective-permute-start.20 = (f32[1,128,512]{2,1,0:T(8,128)}, f32[1,128,512]{2,1,0:T(8,128)}, u32[]{:S(2)}, u32[]{:S(2)}) collective-permute-start(f32[1,128,512]{2,1,0:T(8,128)} %get-tuple-element.98), channel_id=1, source_target_pairs={{0,2},{1,3},{2,0},{3,1},{4,6},{5,7},{6,4},{7,5},{8,10},{9,11},{10,... | collective-permute-start | bytes 786440 | tf_op jit(solution)/shard_map/ppermute | solution.py:334
  144.4 13.7 %collective-permute-start.21 = (f32[1,128,512]{2,1,0:T(8,128)}, f32[1,128,512]{2,1,0:T(8,128)}, u32[]{:S(2)}, u32[]{:S(2)}) collective-permute-start(f32[1,128,512]{2,1,0:T(8,128)} %get-tuple-element.97), channel_id=1, source_target_pairs={{0,3},{1,2},{2,1},{3,0},{4,7},{5,6},{6,5},{7,4},{8,11},{9,10},{10,... | collective-permute-start | bytes 786440 | tf_op jit(solution)/shard_map/ppermute | solution.py:334
  145.8 1.0 copy-start.13
  146.8 1.0 copy-start.15
  147.9 1.0 copy-start.17
  148.9 9.1 %copy-start.1 = (bf16[2,2048,512]{2,1,0:T(8,128)(2,1)S(1)}, bf16[2,2048,512]{2,1,0:T(8,128)(2,1)}, u32[]{:S(2)}) copy-start(bf16[2,2048,512]{2,1,0:T(8,128)(2,1)} %copy-done) | copy-start | bytes 12582916
  148.9 9.1 %copy-start.3 = (bf16[2,2048,512]{2,1,0:T(8,128)(2,1)S(1)}, bf16[2,2048,512]{2,1,0:T(8,128)(2,1)}, u32[]{:S(2)}) copy-start(bf16[2,2048,512]{2,1,0:T(8,128)(2,1)} %copy-done.2) | copy-start | bytes 12582916
  148.9 9.1 %copy-start.9 = (f32[1,512,512]{2,1,0:T(8,128)S(1)}, f32[1,512,512]{2,1,0:T(8,128)}, u32[]{:S(2)}) copy-start(f32[1,512,512]{2,1,0:T(8,128)} %diag_ref.1) | copy-start | bytes 3145732
  153.2 8.6 %copy-start.4 = (f32[8192,128]{1,0:T(8,128)}, f32[8192,128]{1,0:T(8,128)S(1)}, u32[]{:S(2)}) copy-start(f32[8192,128]{1,0:T(8,128)S(1)} %unpack.1.lanes_in) | copy-start | bytes 12582916
  162.0 2.2 %copy-start.5 = (f32[8192,128]{1,0:T(8,128)S(1)}, f32[8192,128]{1,0:T(8,128)}, u32[]{:S(2)}) copy-start(f32[8192,128]{1,0:T(8,128)} %copy-done.4) | copy-start | bytes 12582916

commit v2 on v1

--- a/solution.py
+++ b/solution.py
@@ -14,7 +14,7 @@
 LANES = 128
 SCALE = 16
 VMEM_BYTES = 36 * 1024 * 1024
-LARGE_BYTES = 58 * 1024 * 1024
+MIB = 1024 * 1024
 
 
 def split(x):
@@ -146,7 +146,8 @@
             sent_ref[...] = inner
 
 
-def last_kernel(t, cap, tab, s_ref, third_ref, hi_a, lo_a, hi_b, lo_b, out_ref, message, x_ref):
+def last_kernel(t, cap, tab, s_ref, third_ref, hi_a, lo_a, hi_b, lo_b, *refs):
+    outs, (message, x_ref) = refs[:PLANE], refs[PLANE:]
     rows = third_ref.shape[0]
     padded = s_ref.shape[2]
     me = tab[t.me]
@@ -165,14 +166,15 @@
         def _(flip=flip, hi_ref=hi_ref, lo_ref=lo_ref):
             both = dot(x_ref[...], hi_ref[0])
             product = both[:rows] + both[rows:] + dot(x_ref[:rows, :], lo_ref[0])
-            out_ref[0] = product
+            outs[flip][0] = product
             hot = slots(tab, t, s_ref, me ^ flip, mirror(me, t.blocks), rows, padded) == slot_ids
             hi, lo = split(product)
             part = dot_t(hot.astype(BF16), hi) + dot_t(hot.astype(BF16), lo)
-            if flip == 0:
-                message[...] = part
+            to = slice(flip // 2 * cap, flip // 2 * cap + cap)
+            if flip % 2 == 0:
+                message[to, :] = part
             else:
-                message[...] += part
+                message[to, :] += part
 
 
 def finish_kernel(tab, diag_ref, kept_ref, sibling_ref, other_ref, *refs):
@@ -204,7 +206,7 @@
     return me ^ (3 * PLANE)
 
 
-def store(lanes_ref, t, total, width, child, value, late=False):
+def store(lanes_ref, t, total, width, child, value, late=0):
     lanes = lanes_ref.shape[1]
     for k in range(width // lanes):
         to = pl.ds(k * total + child, total // t.children, stride=t.children)
@@ -212,19 +214,21 @@
         lanes_ref[to, :] = lanes_ref[to, :] + part if late else part
 
 
-def unpack(t, tab, s_ref, lanes_ref, total, message, plane, late=False):
+def unpack(t, tab, s_ref, lanes_ref, total, message, plane, half, late=0):
     cap, width = message.shape
     rows = total // t.children
-    slot_ids = lax.broadcasted_iota(jnp.int32, (rows, cap), 1) + (cap if late else 0)
+    me = tab[t.me]
+    slot_ids = lax.broadcasted_iota(jnp.int32, (rows, cap), 1) + late
     hi, lo = split(message[...])
-    for c in range(PLANE):
-        child = plane * PLANE + c
-        hot = slots(tab, t, s_ref, child, tab[t.me], rows, s_ref.shape[2]) == slot_ids
+    first = plane * PLANE + ((me % PLANE) ^ (2 * half)) // 2 * 2
+    for c in range(2):
+        hot = slots(tab, t, s_ref, first + c, me, rows, s_ref.shape[2]) == slot_ids
         hot = hot.astype(BF16)
-        store(lanes_ref, t, total, width, child, -(dot(hot, hi) + dot(hot, lo)), late)
-
-
-def unpack_kernel(t, tab, s_ref, near_a, near_b, below_ref, above_ref, across_ref, lanes_ref):
+        store(lanes_ref, t, total, width, first + c, -(dot(hot, hi) + dot(hot, lo)), late)
+
+
+def unpack_kernel(t, tab, s_ref, near_a, near_b, *refs):
+    messages, lanes_ref = refs[:-1], refs[-1]
     rows, width = near_a.shape[1:]
     total = rows * t.children
     me = tab[t.me]
@@ -234,32 +238,39 @@
         here = slots(tab, t, s_ref, child, me, rows, s_ref.shape[2]) >= 0
         value = (near_a, near_b)[flip // 2][flip % 2]
         store(lanes_ref, t, total, width, child, jnp.where(here, -value, 0.0))
-
-    @pl.when(z > 0)
-    def _():
-        unpack(t, tab, s_ref, lanes_ref, total, below_ref, z - 1)
-
-    @pl.when(z < PLANES - 1)
-    def _():
-        unpack(t, tab, s_ref, lanes_ref, total, above_ref, z + 1)
-
-    unpack(t, tab, s_ref, lanes_ref, total, across_ref, z ^ 2)
+    for half in range(2):
+        below_ref, above_ref, across_ref = messages[3 * half : 3 * half + 3]
+
+        @pl.when(z > 0)
+        def _(below_ref=below_ref, half=half):
+            unpack(t, tab, s_ref, lanes_ref, total, below_ref, z - 1, half)
+
+        @pl.when(z < PLANES - 1)
+        def _(above_ref=above_ref, half=half):
+            unpack(t, tab, s_ref, lanes_ref, total, above_ref, z + 1, half)
+
+        unpack(t, tab, s_ref, lanes_ref, total, across_ref, z ^ 2, half)
 
 
 def expand_kernel(t, tab, s_ref, message, lanes_in, late_ref, out_ref, late, lanes_ref, sem):
     total, width = out_ref.shape
     lanes = lanes_ref.shape[1]
+    cap, more = message.shape[0] // 2, late.shape[0] // 2
     z = tab[t.me] // PLANE
     at_end = (z == 0) | (z == PLANES - 1)
-    lanes_ref[...] = lanes_in[...]
+    whole = pltpu.make_async_copy(lanes_in, lanes_ref, sem)
+    whole.start()
+    whole.wait()
 
     @pl.when(at_end)
     def _():
-        unpack(t, tab, s_ref, lanes_ref, total, message, z ^ 3)
+        for half in range(2):
+            part = message.at[half * cap : half * cap + cap, :]
+            unpack(t, tab, s_ref, lanes_ref, total, part, z ^ 3, half)
 
     @pl.when(tab[t.over] != 0)
     def _():
-        def more(k, carry):
+        def step(k, carry):
             there = ((k == 0) & (z > 0)) | ((k == 1) & (z < PLANES - 1)) | (k == 2) | ((k == 3) & at_end)
 
             @pl.when(there)
@@ -268,11 +279,13 @@
                 copy.start()
                 copy.wait()
                 plane = jnp.where(k == 0, z - 1, jnp.where(k == 1, z + 1, jnp.where(k == 2, z ^ 2, z ^ 3)))
-                unpack(t, tab, s_ref, lanes_ref, total, late, plane, True)
+                for half in range(2):
+                    part = late.at[half * more : half * more + more, :]
+                    unpack(t, tab, s_ref, lanes_ref, total, part, plane, half, cap)
 
             return carry
 
-        lax.fori_loop(0, PLANE, more, 0)
+        lax.fori_loop(0, PLANE, step, 0)
 
     for k in range(width // lanes):
         out_ref[:, k * lanes : (k + 1) * lanes] = lanes_ref[k * total : (k + 1) * total, :]
@@ -287,18 +300,21 @@
         below(me, t.blocks),
         jnp.where(to == 1, above(me, t.blocks), jnp.where(to == 2, across(me, t.blocks), mirror(me, t.blocks))),
     )
-    slot_ids = lax.broadcasted_iota(jnp.int32, (rows, cap), 1) + cap
+    more = message.shape[1] // 2
+    slot_ids = lax.broadcasted_iota(jnp.int32, (rows, more), 1) + cap
     hot = slots(tab, t, s_ref, me ^ flip, block, rows, s_ref.shape[2]) == slot_ids
     hi, lo = split(values[0, 0])
     part = dot_t(hot.astype(BF16), hi) + dot_t(hot.astype(BF16), lo)
-
-    @pl.when(flip == 0)
-    def _():
-        message[0] = part
-
-    @pl.when(flip != 0)
-    def _():
-        message[0] += part
+    for half in range(2):
+        at = slice(half * more, half * more + more)
+
+        @pl.when(flip == 2 * half)
+        def _(at=at):
+            message[0, at, :] = part
+
+        @pl.when(flip == 2 * half + 1)
+        def _(at=at):
+            message[0, at, :] += part
 
 
 def vmem():
@@ -354,7 +370,7 @@
             out_shape=(shape, shape),
             in_specs=[smem(), vmem()] + [vmem()] * len(given),
             out_specs=(out, out),
-            compiler_params=params(),
+            compiler_params=params(16 * MIB),
             cost_estimate=cost(8 * len(flips) * total * rows * 2 * width, 12 * len(flips) * total * width),
             name="spread",
         )(table, structure3, *given)
@@ -387,7 +403,7 @@
             + [still] * len(partial_sums)
             + [pl.BlockSpec((cap, width), lambda c: (0, 0))] * len(deltas),
             scratch_shapes=[pltpu.VMEM((2 * m, total), BF16)],
-            compiler_params=params(),
+            compiler_params=params(28 * MIB),
             cost_estimate=cost(20 * m * total * width, 4 * len(given) * rows * total + 16 * total * width),
             name="product",
         )(table, structure3, *priors, *given, *panels, *other_products, *factors)
@@ -405,16 +421,16 @@
             functools.partial(last_kernel, t, cap),
             grid=(PLANE,),
             out_shape=(
-                jax.ShapeDtypeStruct((PLANE, rows, width), F32),
-                jax.ShapeDtypeStruct((cap, width), F32),
+                *[jax.ShapeDtypeStruct((1, rows, width), F32)] * PLANE,
+                jax.ShapeDtypeStruct((2 * cap, width), F32),
             ),
             in_specs=[smem()] + [vmem()] * 2 + [a, a, b, b],
             out_specs=(
-                pl.BlockSpec((1, rows, width), lambda c: (c, 0, 0)),
-                pl.BlockSpec((cap, width), lambda c: (0, 0)),
+                *[pl.BlockSpec((1, rows, width), lambda c: (0, 0, 0))] * PLANE,
+                pl.BlockSpec((2 * cap, width), lambda c: (0, 0)),
             ),
             scratch_shapes=[pltpu.VMEM((2 * rows, total), BF16)],
-            compiler_params=params(LARGE_BYTES),
+            compiler_params=params(20 * MIB),
             cost_estimate=cost(40 * rows * total * width, 32 * total * width),
             name="last",
         )(table, structure3, third, *factors_a, *factors_b)
@@ -439,10 +455,10 @@
                 + [factor(flip) for flip in range(PLANE)] * 2,
                 out_specs=first_of,
             ),
-            compiler_params=params(),
+            compiler_params=params(12 * MIB),
             cost_estimate=cost(12 * rows * width * width, 40 * rows * width + 20 * width * width),
             name="finish",
-        )(table, diag_blocks, kept, sibling, other, last, *others, *([factors[0]] * PLANE), *([factors[1]] * PLANE))
+        )(table, diag_blocks, kept, sibling, other, last[0], *others, *([factors[0]] * PLANE), *([factors[1]] * PLANE))
 
     first, second = (0, 1), (2, 3)
     near_to = ((1, below), (2, above))
@@ -463,25 +479,29 @@
         after(across_2, near_a), "row", [(r, r + PLANE if r >= 2 * PLANE else r - PLANE) for r in middle]
     )
     panel_3 = permute(after(panel_2, across_2, near_a), lambda r: r ^ 1)
+    got_below_a = along(up_a, range(PLANES - 1), 1)
+    got_above_a = along(down_a, range(1, PLANES), -1)
     far_a, kept_a, sent_a, twice_a = product(
         first, far, ((0, across),), factors_a, (), (across_2,), True, near, near_a
     )
+    got_across_a = permute(twice_a, lambda r: r ^ (2 * PLANE))
+    early = (got_below_a, got_above_a, got_across_a)
     nearby = (root_inverse, from_below, from_above, across_2)
     hi_b, lo_b, near_b, kept_b, sent_b, down, up, twice = product(
-        second, near + far, near_to + ((3, across),), (), (down_a, up_a, twice_a), nearby, True,
+        second, near + far, near_to + ((3, across),), (), (), nearby, True,
         panels=(after(panel_2, kept_a), panel_3),
     )
     factors_b = (hi_b, lo_b)
     got_across = permute(twice, lambda r: r ^ (2 * PLANE))
     got_below = along(up, range(PLANES - 1), 1)
     got_above = along(down, range(1, PLANES), -1)
-    sibling_a = permute(after(sent_a, mirror_3), lambda r: r ^ 1)
-    sibling_b = permute(after(sent_b, mirror_3), lambda r: r ^ 1)
+    sibling_a = permute(after(sent_a, mirror_3, *early), lambda r: r ^ 1)
+    sibling_b = permute(after(sent_b, mirror_3, *early), lambda r: r ^ 1)
     other = permute(kept_b + sibling_b, lambda r: r ^ 2)
-    last, thrice = final(factors_a, factors_b, after(mirror_3, near_b))
+    *last, thrice = final(factors_a, factors_b, after(mirror_3, near_b))
     got_mirror = mirrored(after(thrice, got_below, got_above, got_across))
     others = [
-        permute(last[flip : flip + 1], functools.partial(lambda flip, r: r ^ flip, flip))
+        permute(last[flip], functools.partial(lambda flip, r: r ^ flip, flip))
         for flip in range(1, PLANE)
     ]
     child_inverse = finish(kept_a, sibling_a, other, last, others, factors_a)
@@ -492,27 +512,29 @@
         functools.partial(unpack_kernel, t),
         grid=(1,),
         out_shape=jax.ShapeDtypeStruct((flat * (width // LANES), LANES), F32),
-        in_specs=[smem(), vmem(), here, here] + [vmem()] * 3,
+        in_specs=[smem(), vmem(), here, here] + [vmem()] * 6,
         out_specs=vmem(),
-        compiler_params=params(),
+        compiler_params=params(16 * MIB),
         cost_estimate=cost(4 * flat * cap * width, 4 * (flat + 5 * cap) * width),
         name="unpack",
-    )(table, structure3, near_a, near_b, got_below, got_above, got_across)
-
-    def late(near_a, far_a, near_b, last):
+    )(table, structure3, near_a, near_b, *early, got_below, got_above, got_across)
+
+    more = 2 * rows - cap
+
+    def late(near_a, far_a, near_b, *last):
         to_below, to_above, to_across = (
             jnp.concatenate([near_a[:, k * rows : (k + 1) * rows] if k < 3 else far_a,
                              near_b[:, k * rows : (k + 1) * rows]])
             for k in (1, 2, 3)
         )
-        values = jnp.stack([to_below, to_above, to_across, last])
+        values = jnp.stack([to_below, to_above, to_across, jnp.concatenate(last)])
         packed = pl.pallas_call(
             functools.partial(late_kernel, t, cap),
             grid=(PLANE, PLANE),
-            out_shape=jax.ShapeDtypeStruct((PLANE, cap, width), F32),
+            out_shape=jax.ShapeDtypeStruct((PLANE, 2 * more, width), F32),
             in_specs=[smem(), vmem(), pl.BlockSpec((1, 1, rows, width), lambda k, c: (k, c, 0, 0))],
-            out_specs=pl.BlockSpec((1, cap, width), lambda k, c: (k, 0, 0)),
-            compiler_params=params(),
+            out_specs=pl.BlockSpec((1, 2 * more, width), lambda k, c: (k, 0, 0)),
+            compiler_params=params(16 * MIB),
             name="late",
         )(table, structure3, values)
         return jnp.stack(
@@ -525,23 +547,23 @@
         )
 
     def none(*unused):
-        return jnp.zeros((PLANE, cap, width), F32)
-
-    more = lax.cond(table[t.over] != 0, late, none, after(near_a, got_mirror, child_inverse, by_lanes), far_a, near_b, last)
+        return jnp.zeros((PLANE, 2 * more, width), F32)
+
+    beyond = lax.cond(table[t.over] != 0, late, none, after(near_a, got_mirror, child_inverse, by_lanes), far_a, near_b, *last)
     block_rows = pl.pallas_call(
         functools.partial(expand_kernel, t),
         out_shape=jax.ShapeDtypeStruct((flat, width), F32),
-        in_specs=[smem()] + [vmem()] * 3 + [pl.BlockSpec(memory_space=pl.ANY)],
+        in_specs=[smem()] + [vmem()] * 2 + [pl.BlockSpec(memory_space=pl.ANY)] * 2,
         out_specs=vmem(),
         scratch_shapes=[
-            pltpu.VMEM((cap, width), F32),
+            pltpu.VMEM((2 * more, width), F32),
             pltpu.VMEM((flat * (width // LANES), LANES), F32),
             pltpu.SemaphoreType.DMA,
         ],
-        compiler_params=params(),
+        compiler_params=params(16 * MIB),
         cost_estimate=cost(flat * cap * width, 8 * flat * width),
         name="expand",
-    )(table, structure3, got_mirror, after(by_lanes, child_inverse), more)
+    )(table, structure3, got_mirror, after(by_lanes, child_inverse), beyond)
     return block_rows.reshape(rows, children, width), child_inverse
 
 
@@ -553,13 +575,10 @@
     block_of = jnp.where(positions[None, :] < live[:, None], structure // rows, blocks)
     edges = jnp.arange(blocks + 1, dtype=jnp.int32)
     first = jnp.sum((block_of[:, None, :] < edges[None, :, None]).astype(jnp.int32), axis=2)
-    counts = (first[:, 1:] - first[:, :-1]).reshape(PLANES, PLANE, blocks)
-    offsets = [jnp.zeros_like(counts[:, 0])]
-    for c in range(PLANE):
-        offsets.append(offsets[-1] + counts[:, c])
-    largest = jnp.max(offsets[-1])
-    offset = jnp.stack(offsets[:-1], axis=1).reshape(children, blocks)
-    cap = 2 * rows
+    counts = (first[:, 1:] - first[:, :-1]).reshape(children // 2, 2, blocks)
+    largest = jnp.max(counts[:, 0] + counts[:, 1])
+    offset = jnp.stack([jnp.zeros_like(counts[:, 0]), counts[:, 0]], axis=1).reshape(children, blocks)
+    cap = rows + rows // 8
     table = jnp.concatenate(
         [
             first[:, :-1].reshape(-1),

time: 170 us -> 161 us (0.947)
  waiting for transfers between devices: 51.6 us -> 40.5 us
  starting transfers between devices: 32 us -> 40.6 us
  Pallas kernels: 66.3 us -> 58.8 us
    ppermute x10 -> x11, waiting for transfers between devices: 29.4 us -> 13.7 us  [permute(): return lax.ppermute(x, 'row', [(r, move(r)) for r in range(blocks)])]
    ppermute x10 -> x11, starting transfers between devices: 12.7 us -> 20 us  [permute(): return lax.ppermute(x, 'row', [(r, move(r)) for r in range(blocks)])]
    pallas_call x1, Pallas kernels: 11.6 us -> 6.8 us  [final(): pl.pallas_call(functools.partial(last_kernel, t, cap), grid=(PLANE,), out...]
    ppermute x6 -> x8, waiting for transfers between devices: 22.2 us -> 26.7 us  [along(): lax.ppermute(x, 'row', [(p * PLANE + b, (p + step) * PLANE + b) for p in...]
    pallas_call x3, Pallas kernels: 35.1 us -> 32 us  [product(): pl.pallas_call(functools.partial(product_kernel, t, flips, here, there, s...]
    unnamed x40 -> x42, local copies, waits for them, and re-layouts: 10.1 us -> 12.9 us
    slice x1 -> x0, local copies, waits for them, and re-layouts: 2.13 us -> none  [planes_body(): last[flip:flip + 1]]
    ppermute x6 -> x8, starting transfers between devices: 15.9 us -> 17.4 us  [along(): lax.ppermute(x, 'row', [(p * PLANE + b, (p + step) * PLANE + b) for p in...]
  transfers between devices with their start and end apart: 18 -> 21, of which waited for: 5 -> 6; matrix products, arithmetic and copies ran while one was open for 4% -> 3% of each run, Pallas kernels for 36% -> 34%
where the time goes in v2:
time: 161 us; the launch traced here: 160 us
  Pallas kernels  58.8 us (37%)
  starting transfers between devices  40.6 us (25%)
  waiting for transfers between devices  40.5 us (25%)
  local copies, waits for them, and re-layouts  15 us (9%)
  other arithmetic  3.26 us (2%)
  between operations  1.74 us (1%)
    pallas_call x3, Pallas kernels, product(): pl.pallas_call(functools.partial(product_kernel, t, flips, here, there, s...  32 us
    ppermute x8, waiting for transfers between devices, along(): lax.ppermute(x, 'row', [(p * PLANE + b, (p + step) * PLANE + b) for p in...  26.7 us
    ppermute x11, starting transfers between devices, permute(): return lax.ppermute(x, 'row', [(r, move(r)) for r in range(blocks)])  20 us
    ppermute x8, starting transfers between devices, along(): lax.ppermute(x, 'row', [(p * PLANE + b, (p + step) * PLANE + b) for p in...  17.4 us
    ppermute x11, waiting for transfers between devices, permute(): return lax.ppermute(x, 'row', [(r, move(r)) for r in range(blocks)])  13.7 us
    unnamed x42, local copies, waits for them, and re-layouts  12.9 us
    pallas_call x1, Pallas kernels, final(): pl.pallas_call(functools.partial(last_kernel, t, cap), grid=(PLANE,), out...  6.8 us
    pallas_call x1, Pallas kernels, spread(): pl.pallas_call(functools.partial(spread_kernel, t, flips, unroll), grid=(...  6.62 us
  transfers between devices with their start and end apart: 21, of which 6 were waited for; matrix products, arithmetic and copies ran while one was open for 3% of the time, Pallas kernels for 34%

profile of v2, /device:TPU:1, one launch (start us, length us, event | category | flops | bytes accessed | tf_op | source)
XLA Modules:
  0.0 159.9 jit_solution(10239523293546284215)
XLA Ops:
  0.8 1.3 collective-permute-start.7
  2.0 5.3 %collective-permute-start.4 = (f32[128,2048]{1,0:T(8,128)}, f32[128,2048]{1,0:T(8,128)S(1)}, u32[]{:S(2)}, u32[]{:S(2)}) collective-permute-start(f32[128,2048]{1,0:T(8,128)} %refs_0_.5), channel_id=1, source_target_pairs={{0,4},{1,5},{2,6},{3,7},{4,8},{5,9},{6,10},{7,11},{8,12},{9,13},{1... | collective-permute-start | bytes 3145736 | tf_op jit(solution)/shard_map/ppermute | solution.py:353
  7.4 1.5 collective-permute-start.10
  8.9 0.9 reshape.21.s_ref
  9.7 0.9 fusion.1
  11.1 0.6 reduce_max.9
  12.7 0.7 concatenate.15.tab
  13.4 1.7 %copy-done.7 = f32[1,1024,512]{2,1,0:T(8,128)S(1)} copy-done((f32[1,1024,512]{2,1,0:T(8,128)S(1)}, f32[1,1024,512]{2,1,0:T(8,128)}, u32[]{:S(2)}) %copy-start.7) | copy-done | bytes 2097176
  15.1 6.6 %spread.1 = (bf16[2,2048,512]{2,1,0:T(8,128)(2,1)S(1)}, bf16[2,2048,512]{2,1,0:T(8,128)(2,1)S(1)}) custom-call(s32[530]{0:T(1024)S(1)} %concatenate.15.tab, s32[16,1,1024]{2,1,0:T(1,128)S(1)} %reshape.21.s_ref, f32[1,1024,512]{2,1,0:T(8,128)S(1)} %copy-done.7, f32[1,1024,512]{2,1,0:T(8,128)} %collective-permute-done.5.refs_1_), custom_call_target="tpu_custom_call" | custom-call | flops 268435456 | bytes 1572864 | tf_op jit(solution)/shard_map/spread/pallas_call | solution.py:367
  21.8 7.4 %collective-permute-done.7.refs_2_ = f32[128,2048]{1,0:T(8,128)S(1)} collective-permute-done((f32[128,2048]{1,0:T(8,128)}, f32[128,2048]{1,0:T(8,128)S(1)}, u32[]{:S(2)}, u32[]{:S(2)}) %collective-permute-start.7) | collective-permute-done | bytes 1048608 | tf_op jit(solution)/shard_map/ppermute | solution.py:353
  29.2 1.3 collective-permute-start.8
  30.5 0.7 collective-permute-start.6
  31.3 7.5 %product.3 = (f32[2,384,512]{2,1,0:T(8,128)S(1)}, f32[144,512]{1,0:T(8,128)S(1)}, f32[144,512]{1,0:T(8,128)S(1)}) custom-call(s32[530]{0:T(1024)S(1)} %concatenate.15.tab, s32[16,1,1024]{2,1,0:T(1,128)S(1)} %reshape.21.s_ref, f32[128,2048]{1,0:T(8,128)S(1)} %copy-done.6, f32[128,2048]{1,0:T(8,128)S(1)} %collective-permute-done.4.refs_1_, ...), custom_call_target="tpu_custom_call" | custom-call | flops 503316480 | bytes 1245184 | tf_op jit(solution)/shard_map/product/pallas_call | solution.py:388
  38.8 16.6 %collective-permute-done.8 = f32[128,2048]{1,0:T(8,128)S(1)} collective-permute-done((f32[128,2048]{1,0:T(8,128)S(1)}, f32[128,2048]{1,0:T(8,128)S(1)}, u32[]{:S(2)}, u32[]{:S(2)}) %collective-permute-start.8) | collective-permute-done | bytes 1048608 | tf_op jit(solution)/shard_map/ppermute | solution.py:353
  55.6 1.3 collective-permute-start.11
  56.9 1.3 collective-permute-start.9
  58.2 4.5 %collective-permute-start.16 = (f32[144,512]{1,0:T(8,128)S(1)}, f32[144,512]{1,0:T(8,128)S(1)}, u32[]{:S(2)}, u32[]{:S(2)}) collective-permute-start(f32[144,512]{1,0:T(8,128)S(1)} %get-tuple-element.83), channel_id=1, source_target_pairs={{0,4},{1,5},{2,6},{3,7},{4,8},{5,9},{6,10},{7,11},{8,12},{9,13},{1... | collective-permute-start | bytes 884744 | tf_op jit(solution)/shard_map/ppermute | solution.py:353
  62.7 1.5 collective-permute-start.17
  64.1 6.0 %product.4 = (f32[2,128,512]{2,1,0:T(8,128)}, f32[512,512]{1,0:T(8,128)S(1)}, f32[512,512]{1,0:T(8,128)S(1)}, f32[144,512]{1,0:T(8,128)S(1)}) custom-call(s32[530]{0:T(1024)S(1)} %concatenate.15.tab, s32[16,1,1024]{2,1,0:T(1,128)S(1)} %reshape.21.s_ref, f32[128,2048]{1,0:T(8,128)S(1)} %add.14.refs_0_.refs_3_, ...), custom_call_target="tpu_custom_call" | custom-call | flops 167772160 | bytes 1114112 | tf_op jit(solution)/shard_map/product/pallas_call | solution.py:388
  70.2 5.6 %collective-permute-start.18 = (f32[144,512]{1,0:T(8,128)S(1)}, f32[144,512]{1,0:T(8,128)S(1)}, u32[]{:S(2)}, u32[]{:S(2)}) collective-permute-start(f32[144,512]{1,0:T(8,128)S(1)} %get-tuple-element.85), channel_id=1, source_target_pairs={{0,8},{1,9},{2,10},{3,11},{4,12},{5,13},{6,14},{7,15},{8,0},{9,1},... | collective-permute-start | bytes 884744 | tf_op jit(solution)/shard_map/ppermute | solution.py:350
  75.7 18.4 %product.5 = (bf16[2,2048,512]{2,1,0:T(8,128)(2,1)S(1)}, bf16[2,2048,512]{2,1,0:T(8,128)(2,1)S(1)}, f32[2,512,512]{2,1,0:T(8,128)}, f32[512,512]{1,0:T(8,128)S(1...) custom-call(s32[530]{0:T(1024)S(1)} %concatenate.15.tab, ...), custom_call_target="tpu_custom_call" | custom-call | flops 671088640 | bytes 1310720 | tf_op jit(solution)/shard_map/product/pallas_call | solution.py:388
  94.2 2.6 %collective-permute-done.17.refs_1_ = f32[144,512]{1,0:T(8,128)S(1)} collective-permute-done((f32[144,512]{1,0:T(8,128)S(1)}, f32[144,512]{1,0:T(8,128)S(1)}, u32[]{:S(2)}, u32[]{:S(2)}) %collective-permute-start.17) | collective-permute-done | bytes 294944 | tf_op jit(solution)/shard_map/ppermute | solution.py:353
  96.8 0.7 collective-permute-start.20
  97.5 2.2 %collective-permute-done.20 = f32[512,512]{1,0:T(8,128)S(1)} collective-permute-done((f32[512,512]{1,0:T(8,128)S(1)}, f32[512,512]{1,0:T(8,128)S(1)}, u32[]{:S(2)}, u32[]{:S(2)}) %collective-permute-start.20) | collective-permute-done | bytes 1048608 | tf_op jit(solution)/shard_map/ppermute | solution.py:350
  99.8 1.2 add.15
  100.9 1.2 collective-permute-start.21
  102.2 1.3 collective-permute-start.12
  103.5 1.5 collective-permute-start.13
  105.0 6.3 %collective-permute-start.14 = (f32[144,512]{1,0:T(8,128)S(1)}, f32[144,512]{1,0:T(8,128)S(1)}, u32[]{:S(2)}, u32[]{:S(2)}) collective-permute-start(f32[144,512]{1,0:T(8,128)S(1)} %get-tuple-element.81), channel_id=1, source_target_pairs={{0,8},{1,9},{2,10},{3,11},{4,12},{5,13},{6,14},{7,15},{8,0},{9,1},... | collective-permute-start | bytes 884744 | tf_op jit(solution)/shard_map/ppermute | solution.py:350
  111.3 6.8 %last.1 = (f32[1,128,512]{2,1,0:T(8,128)}, f32[1,128,512]{2,1,0:T(8,128)}, f32[1,128,512]{2,1,0:T(8,128)}, f32[1,128,512]{2,1,0:T(8,128)}, f32[288,512]{1,0:T(8,128)}) custom-call(s32[530]{0:T(1024)S(1)} %concatenate.15.tab, s32[16,1,1024]{2,1,0:T(1,128)S(1)} %reshape.21.s_ref, f32[128,2048]{1,0:T(8,128)S(1)} %collective-permute-done.9.third_ref, ...), custom_call_target="tpu_custom_call" | custom-call | flops 335544320 | bytes 2097152 | tf_op jit(solution)/shard_map/last/pallas_call | solution.py:420
  118.1 0.7 copy-done.13
  118.8 0.7 copy-done.15
  119.5 10.5 %collective-permute-done.14.refs_5_ = f32[144,512]{1,0:T(8,128)S(1)} collective-permute-done((f32[144,512]{1,0:T(8,128)S(1)}, f32[144,512]{1,0:T(8,128)S(1)}, u32[]{:S(2)}, u32[]{:S(2)}) %collective-permute-start.14) | collective-permute-done | bytes 294944 | tf_op jit(solution)/shard_map/ppermute | solution.py:350
  130.0 0.7 copy-done.17
  130.8 1.9 %collective-permute-start.15 = (f32[288,512]{1,0:T(8,128)}, f32[288,512]{1,0:T(8,128)}, u32[]{:S(2)}, u32[]{:S(2)}) collective-permute-start(f32[288,512]{1,0:T(8,128)} %get-tuple-element.82), channel_id=1, source_target_pairs={{0,12},{1,13},{2,14},{3,15},{12,0},{13,1},{14,2},{15,3},{16,28},{1... | collective-permute-start | bytes 1769480 | tf_op jit(solution)/shard_map/ppermute | solution.py:359
  132.7 1.6 collective-permute-start.22
  134.5 1.5 collective-permute-start.24
  136.0 1.0 copy-done.10
  136.9 1.0 copy-done.12
  137.9 1.0 copy-done.14
  138.9 1.0 copy-done.16
  139.8 1.0 copy-done.18
  140.8 4.7 %unpack.1.lanes_in = f32[8192,128]{1,0:T(8,128)S(1)} custom-call(s32[530]{0:T(1024)S(1)} %concatenate.15.tab, s32[16,1,1024]{2,1,0:T(1,128)S(1)} %reshape.21.s_ref, f32[2,384,512]{2,1,0:T(8,128)} %copy-done.19, f32[2,512,512]{2,1,0:T(8,128)} %get-tuple-element.74.near_b, f32[144,512]{1,0:T(8,128)S(1)} %collective-permute-done.16.refs_0_, ...), custom_call_target="tpu_custom_call" | custom-call | flops 37748736 | bytes 354304 | tf_op jit(solution)/shard_map/unpack/pallas_call | solution.py:511
  145.5 2.0 %copy-done.4 = f32[8192,128]{1,0:T(8,128)} copy-done((f32[8192,128]{1,0:T(8,128)}, f32[8192,128]{1,0:T(8,128)S(1)}, u32[]{:S(2)}) %copy-start.4) | copy-done | bytes 4194328
  147.5 1.0 collective-permute-done.24.refs_3_
  148.6 3.7 %finish.1 = f32[1,512,512]{2,1,0:T(8,128)} custom-call(s32[530]{0:T(1024)S(1)} %concatenate.15.tab, f32[1,512,512]{2,1,0:T(8,128)S(1)} %copy-done.8, f32[512,512]{1,0:T(8,128)S(1)} %get-tuple-element.71.kept_ref, f32[512,512]{1,0:T(8,128)S(1)} %collective-permute-done.19.sibling_ref, f32[512,512]{1,0:T(8,128)S(1)} %collective-permute-done.21.other_ref, ...), custom_call_target="tpu_custom_call" | custom-call | flops 25165824 | bytes 491520 | tf_op jit(solution)/shard_map/finish/pallas_call | solution.py:446
  152.5 2.2 %copy-done.5 = f32[8192,128]{1,0:T(8,128)S(1)} copy-done((f32[8192,128]{1,0:T(8,128)S(1)}, f32[8192,128]{1,0:T(8,128)}, u32[]{:S(2)}) %copy-start.5) | copy-done | bytes 4194328
  154.7 5.1 %expand.1 = f32[2048,512]{1,0:T(8,128)} custom-call(s32[530]{0:T(1024)S(1)} %concatenate.15.tab, s32[16,1,1024]{2,1,0:T(1,128)S(1)} %reshape.21.s_ref, f32[288,512]{1,0:T(8,128)} %collective-permute-done.15.message, f32[8192,128]{1,0:T(8,128)S(1)} %copy-done.5, f32[4,224,512]{2,1,0:T(8,128)S(1)} %get-tuple-element.115.late_ref), custom_call_target="tpu_custom_call" | custom-call | flops 9437184 | bytes 524288 | tf_op jit(solution)/shard_map/expand/pallas_call | solution.py:553
  (60 shorter events, 1.8 us)
Async XLA Ops:
  0.6 12.8 %collective-permute-start.5 = (f32[1,1024,512]{2,1,0:T(8,128)}, f32[1,1024,512]{2,1,0:T(8,128)}, u32[]{:S(2)}, u32[]{:S(2)}) collective-permute-start(f32[1,1024,512]{2,1,0:T(8,128)} %refs_0_.3), channel_id=1, source_target_pairs={{0,1},{1,0},{2,3},{3,2},{4,5},{5,4},{6,7},{7,6},{8,9},{9,8},{10,11... | collective-permute-start | bytes 6291464 | tf_op jit(solution)/shard_map/ppermute | solution.py:350
  0.8 28.5 %collective-permute-start.7 = (f32[128,2048]{1,0:T(8,128)}, f32[128,2048]{1,0:T(8,128)S(1)}, u32[]{:S(2)}, u32[]{:S(2)}) collective-permute-start(f32[128,2048]{1,0:T(8,128)} %refs_0_.5), channel_id=1, source_target_pairs={{4,0},{5,1},{6,2},{7,3},{8,4},{9,5},{10,6},{11,7},{12,8},{13,9},{1... | collective-permute-start | bytes 3145736 | tf_op jit(solution)/shard_map/ppermute | solution.py:353
  2.0 28.5 %collective-permute-start.4 = (f32[128,2048]{1,0:T(8,128)}, f32[128,2048]{1,0:T(8,128)S(1)}, u32[]{:S(2)}, u32[]{:S(2)}) collective-permute-start(f32[128,2048]{1,0:T(8,128)} %refs_0_.5), channel_id=1, source_target_pairs={{0,4},{1,5},{2,6},{3,7},{4,8},{5,9},{6,10},{7,11},{8,12},{9,13},{1... | collective-permute-start | bytes 3145736 | tf_op jit(solution)/shard_map/ppermute | solution.py:353
  7.4 48.2 %collective-permute-start.10 = (f32[1,1024,512]{2,1,0:T(8,128)}, f32[1,1024,512]{2,1,0:T(8,128)}, u32[]{:S(2)}, u32[]{:S(2)}) collective-permute-start(f32[1,1024,512]{2,1,0:T(8,128)} %refs_0_.3), channel_id=1, source_target_pairs={{0,2},{1,3},{2,0},{3,1},{4,6},{5,7},{6,4},{7,5},{8,10},{9,11},{10,... | collective-permute-start | bytes 6291464 | tf_op jit(solution)/shard_map/ppermute | solution.py:350
  13.4 17.8 %copy-start.6 = (f32[128,2048]{1,0:T(8,128)S(1)}, f32[128,2048]{1,0:T(8,128)}, u32[]{:S(2)}) copy-start(f32[128,2048]{1,0:T(8,128)} %refs_0_.5) | copy-start | bytes 3145732
  13.4 1.7 %copy-start.7 = (f32[1,1024,512]{2,1,0:T(8,128)S(1)}, f32[1,1024,512]{2,1,0:T(8,128)}, u32[]{:S(2)}) copy-start(f32[1,1024,512]{2,1,0:T(8,128)} %refs_0_.3) | copy-start | bytes 6291460
  21.8 89.5 %copy-start = (bf16[2,2048,512]{2,1,0:T(8,128)(2,1)}, bf16[2,2048,512]{2,1,0:T(8,128)(2,1)S(1)}, u32[]{:S(2)}) copy-start(bf16[2,2048,512]{2,1,0:T(8,128)(2,1)S(1)} %get-tuple-element.65.refs_3_.refs_2_.hi_a.refs_4_.refs_5_.refs_6_.refs_7_) | copy-start | bytes 12582916
  21.8 89.5 %copy-start.2 = (bf16[2,2048,512]{2,1,0:T(8,128)(2,1)}, bf16[2,2048,512]{2,1,0:T(8,128)(2,1)S(1)}, u32[]{:S(2)}) copy-start(bf16[2,2048,512]{2,1,0:T(8,128)(2,1)S(1)} %get-tuple-element.66.refs_4_.refs_3_.lo_a.refs_8_.refs_9_.refs_10_.refs_11_) | copy-start | bytes 12582916
  29.2 26.2 %collective-permute-start.8 = (f32[128,2048]{1,0:T(8,128)S(1)}, f32[128,2048]{1,0:T(8,128)S(1)}, u32[]{:S(2)}, u32[]{:S(2)}) collective-permute-start(f32[128,2048]{1,0:T(8,128)S(1)} %collective-permute-done.7.refs_2_), channel_id=1, source_target_pairs={{4,0},{5,1},{6,2},{7,3},{8,4},{9,5},{10,6},{11,7},{20,16},{21,17},... | collective-permute-start | bytes 3145736 | tf_op jit(solution)/shard_map/ppermute | solution.py:353
  30.5 24.9 %collective-permute-start.6 = (f32[128,2048]{1,0:T(8,128)S(1)}, f32[128,2048]{1,0:T(8,128)S(1)}, u32[]{:S(2)}, u32[]{:S(2)}) collective-permute-start(f32[128,2048]{1,0:T(8,128)S(1)} %collective-permute-done.4.refs_1_), channel_id=1, source_target_pairs={{4,8},{5,9},{6,10},{7,11},{8,12},{9,13},{10,14},{11,15},{20,24},{2... | collective-permute-start | bytes 3145736 | tf_op jit(solution)/shard_map/ppermute | solution.py:353
  38.8 31.4 %copy-start.19 = (f32[2,384,512]{2,1,0:T(8,128)}, f32[2,384,512]{2,1,0:T(8,128)S(1)}, u32[]{:S(2)}) copy-start(f32[2,384,512]{2,1,0:T(8,128)S(1)} %get-tuple-element.96.refs_1_.near_a) | copy-start | bytes 4718596
  55.6 20.2 %collective-permute-start.11 = (f32[1,1024,512]{2,1,0:T(8,128)}, f32[1,1024,512]{2,1,0:T(8,128)S(1)}, u32[]{:S(2)}, u32[]{:S(2)}) collective-permute-start(f32[1,1024,512]{2,1,0:T(8,128)} %collective-permute-done.10.refs_4_), channel_id=1, source_target_pairs={{0,1},{1,0},{2,3},{3,2},{4,5},{5,4},{6,7},{7,6},{8,9},{9,8},{10,11... | collective-permute-start | bytes 6291464 | tf_op jit(solution)/shard_map/ppermute | solution.py:350
  56.9 39.9 %collective-permute-start.9 = (f32[128,2048]{1,0:T(8,128)S(1)}, f32[128,2048]{1,0:T(8,128)S(1)}, u32[]{:S(2)}, u32[]{:S(2)}) collective-permute-start(f32[128,2048]{1,0:T(8,128)S(1)} %add.14.refs_0_.refs_3_), channel_id=1, source_target_pairs={{4,0},{5,1},{6,2},{7,3},{8,12},{9,13},{10,14},{11,15},{20,16},{21,... | collective-permute-start | bytes 3145736 | tf_op jit(solution)/shard_map/ppermute | solution.py:478
  58.2 36.0 %collective-permute-start.16 = (f32[144,512]{1,0:T(8,128)S(1)}, f32[144,512]{1,0:T(8,128)S(1)}, u32[]{:S(2)}, u32[]{:S(2)}) collective-permute-start(f32[144,512]{1,0:T(8,128)S(1)} %get-tuple-element.83), channel_id=1, source_target_pairs={{0,4},{1,5},{2,6},{3,7},{4,8},{5,9},{6,10},{7,11},{8,12},{9,13},{1... | collective-permute-start | bytes 884744 | tf_op jit(solution)/shard_map/ppermute | solution.py:353
  62.7 34.1 %collective-permute-start.17 = (f32[144,512]{1,0:T(8,128)S(1)}, f32[144,512]{1,0:T(8,128)S(1)}, u32[]{:S(2)}, u32[]{:S(2)}) collective-permute-start(f32[144,512]{1,0:T(8,128)S(1)} %get-tuple-element.84), channel_id=1, source_target_pairs={{4,0},{5,1},{6,2},{7,3},{8,4},{9,5},{10,6},{11,7},{12,8},{13,9},{1... | collective-permute-start | bytes 884744 | tf_op jit(solution)/shard_map/ppermute | solution.py:353
  70.2 26.6 %collective-permute-start.18 = (f32[144,512]{1,0:T(8,128)S(1)}, f32[144,512]{1,0:T(8,128)S(1)}, u32[]{:S(2)}, u32[]{:S(2)}) collective-permute-start(f32[144,512]{1,0:T(8,128)S(1)} %get-tuple-element.85), channel_id=1, source_target_pairs={{0,8},{1,9},{2,10},{3,11},{4,12},{5,13},{6,14},{7,15},{8,0},{9,1},... | collective-permute-start | bytes 884744 | tf_op jit(solution)/shard_map/ppermute | solution.py:350
  96.8 21.3 %copy-start.9 = (f32[144,512]{1,0:T(8,128)}, f32[144,512]{1,0:T(8,128)S(1)}, u32[]{:S(2)}) copy-start(f32[144,512]{1,0:T(8,128)S(1)} %collective-permute-done.17.refs_1_) | copy-start | bytes 884740
  96.8 21.3 %copy-start.11 = (f32[144,512]{1,0:T(8,128)}, f32[144,512]{1,0:T(8,128)S(1)}, u32[]{:S(2)}) copy-start(f32[144,512]{1,0:T(8,128)S(1)} %collective-permute-done.18.refs_2_) | copy-start | bytes 884740
  96.8 3.0 %collective-permute-start.20 = (f32[512,512]{1,0:T(8,128)S(1)}, f32[512,512]{1,0:T(8,128)S(1)}, u32[]{:S(2)}, u32[]{:S(2)}) collective-permute-start(f32[512,512]{1,0:T(8,128)S(1)} %get-tuple-element.90), channel_id=1, source_target_pairs={{0,1},{1,0},{2,3},{3,2},{4,5},{5,4},{6,7},{7,6},{8,9},{9,8},{10,11... | collective-permute-start | bytes 3145736 | tf_op jit(solution)/shard_map/ppermute | solution.py:350
  97.5 37.0 %collective-permute-start.19 = (f32[512,512]{1,0:T(8,128)S(1)}, f32[512,512]{1,0:T(8,128)S(1)}, u32[]{:S(2)}, u32[]{:S(2)}) collective-permute-start(f32[512,512]{1,0:T(8,128)S(1)} %get-tuple-element.87), channel_id=1, source_target_pairs={{0,1},{1,0},{2,3},{3,2},{4,5},{5,4},{6,7},{7,6},{8,9},{9,8},{10,11... | collective-permute-start | bytes 3145736 | tf_op jit(solution)/shard_map/ppermute | solution.py:350
  100.9 47.6 %collective-permute-start.21 = (f32[512,512]{1,0:T(8,128)}, f32[512,512]{1,0:T(8,128)S(1)}, u32[]{:S(2)}, u32[]{:S(2)}) collective-permute-start(f32[512,512]{1,0:T(8,128)} %add.15), channel_id=1, source_target_pairs={{0,2},{1,3},{2,0},{3,1},{4,6},{5,7},{6,4},{7,5},{8,10},{9,11},{10,... | collective-permute-start | bytes 3145736 | tf_op jit(solution)/shard_map/ppermute | solution.py:350
  102.2 15.9 %collective-permute-start.12 = (f32[144,512]{1,0:T(8,128)S(1)}, f32[144,512]{1,0:T(8,128)S(1)}, u32[]{:S(2)}, u32[]{:S(2)}) collective-permute-start(f32[144,512]{1,0:T(8,128)S(1)} %get-tuple-element.79), channel_id=1, source_target_pairs={{0,4},{1,5},{2,6},{3,7},{4,8},{5,9},{6,10},{7,11},{8,12},{9,13},{1... | collective-permute-start | bytes 884744 | tf_op jit(solution)/shard_map/ppermute | solution.py:353
  103.5 15.3 %collective-permute-start.13 = (f32[144,512]{1,0:T(8,128)S(1)}, f32[144,512]{1,0:T(8,128)S(1)}, u32[]{:S(2)}, u32[]{:S(2)}) collective-permute-start(f32[144,512]{1,0:T(8,128)S(1)} %get-tuple-element.80), channel_id=1, source_target_pairs={{4,0},{5,1},{6,2},{7,3},{8,4},{9,5},{10,6},{11,7},{12,8},{13,9},{1... | collective-permute-start | bytes 884744 | tf_op jit(solution)/shard_map/ppermute | solution.py:353
  105.0 25.0 %collective-permute-start.14 = (f32[144,512]{1,0:T(8,128)S(1)}, f32[144,512]{1,0:T(8,128)S(1)}, u32[]{:S(2)}, u32[]{:S(2)}) collective-permute-start(f32[144,512]{1,0:T(8,128)S(1)} %get-tuple-element.81), channel_id=1, source_target_pairs={{0,8},{1,9},{2,10},{3,11},{4,12},{5,13},{6,14},{7,15},{8,0},{9,1},... | collective-permute-start | bytes 884744 | tf_op jit(solution)/shard_map/ppermute | solution.py:350
  118.1 0.7 copy-start.13
  118.8 0.7 copy-start.15
  130.0 0.7 copy-start.17
  130.8 21.5 %collective-permute-start.15 = (f32[288,512]{1,0:T(8,128)}, f32[288,512]{1,0:T(8,128)}, u32[]{:S(2)}, u32[]{:S(2)}) collective-permute-start(f32[288,512]{1,0:T(8,128)} %get-tuple-element.82), channel_id=1, source_target_pairs={{0,12},{1,13},{2,14},{3,15},{12,0},{13,1},{14,2},{15,3},{16,28},{1... | collective-permute-start | bytes 1769480 | tf_op jit(solution)/shard_map/ppermute | solution.py:359
  132.7 14.9 %collective-permute-start.22 = (f32[1,128,512]{2,1,0:T(8,128)}, f32[1,128,512]{2,1,0:T(8,128)}, u32[]{:S(2)}, u32[]{:S(2)}) collective-permute-start(f32[1,128,512]{2,1,0:T(8,128)} %get-tuple-element.92), channel_id=1, source_target_pairs={{0,1},{1,0},{2,3},{3,2},{4,5},{5,4},{6,7},{7,6},{8,9},{9,8},{10,11... | collective-permute-start | bytes 786440 | tf_op jit(solution)/shard_map/ppermute | solution.py:350
  134.3 13.3 %collective-permute-start.23 = (f32[1,128,512]{2,1,0:T(8,128)}, f32[1,128,512]{2,1,0:T(8,128)}, u32[]{:S(2)}, u32[]{:S(2)}) collective-permute-start(f32[1,128,512]{2,1,0:T(8,128)} %get-tuple-element.93), channel_id=1, source_target_pairs={{0,2},{1,3},{2,0},{3,1},{4,6},{5,7},{6,4},{7,5},{8,10},{9,11},{10,... | collective-permute-start | bytes 786440 | tf_op jit(solution)/shard_map/ppermute | solution.py:350
  134.5 14.0 %collective-permute-start.24 = (f32[1,128,512]{2,1,0:T(8,128)}, f32[1,128,512]{2,1,0:T(8,128)}, u32[]{:S(2)}, u32[]{:S(2)}) collective-permute-start(f32[1,128,512]{2,1,0:T(8,128)} %get-tuple-element.94), channel_id=1, source_target_pairs={{0,3},{1,2},{2,1},{3,0},{4,7},{5,6},{6,5},{7,4},{8,11},{9,10},{10,... | collective-permute-start | bytes 786440 | tf_op jit(solution)/shard_map/ppermute | solution.py:350
  136.0 1.0 copy-start.10
  136.9 1.0 copy-start.12
  137.9 1.0 copy-start.14
  138.9 1.0 copy-start.16
  139.8 1.0 copy-start.18
  140.8 7.8 %copy-start.1 = (bf16[2,2048,512]{2,1,0:T(8,128)(2,1)S(1)}, bf16[2,2048,512]{2,1,0:T(8,128)(2,1)}, u32[]{:S(2)}) copy-start(bf16[2,2048,512]{2,1,0:T(8,128)(2,1)} %copy-done) | copy-start | bytes 12582916
  140.8 7.8 %copy-start.3 = (bf16[2,2048,512]{2,1,0:T(8,128)(2,1)S(1)}, bf16[2,2048,512]{2,1,0:T(8,128)(2,1)}, u32[]{:S(2)}) copy-start(bf16[2,2048,512]{2,1,0:T(8,128)(2,1)} %copy-done.2) | copy-start | bytes 12582916
  140.8 7.8 %copy-start.8 = (f32[1,512,512]{2,1,0:T(8,128)S(1)}, f32[1,512,512]{2,1,0:T(8,128)}, u32[]{:S(2)}) copy-start(f32[1,512,512]{2,1,0:T(8,128)} %diag_ref.1) | copy-start | bytes 3145732
  140.8 7.8 %copy-start.21 = (f32[1,128,512]{2,1,0:T(8,128)S(1)}, f32[1,128,512]{2,1,0:T(8,128)}, u32[]{:S(2)}) copy-start(f32[1,128,512]{2,1,0:T(8,128)} %get-tuple-element.91.refs_0_) | copy-start | bytes 786436
  145.5 2.0 %copy-start.4 = (f32[8192,128]{1,0:T(8,128)}, f32[8192,128]{1,0:T(8,128)S(1)}, u32[]{:S(2)}) copy-start(f32[8192,128]{1,0:T(8,128)S(1)} %unpack.1.lanes_in) | copy-start | bytes 12582916
  152.5 2.2 %copy-start.5 = (f32[8192,128]{1,0:T(8,128)S(1)}, f32[8192,128]{1,0:T(8,128)}, u32[]{:S(2)}) copy-start(f32[8192,128]{1,0:T(8,128)} %copy-done.4) | copy-start | bytes 12582916

commit v3 on v2

--- a/solution.py
+++ b/solution.py
@@ -492,14 +492,14 @@
         panels=(after(panel_2, kept_a), panel_3),
     )
     factors_b = (hi_b, lo_b)
-    got_across = permute(twice, lambda r: r ^ (2 * PLANE))
     got_below = along(up, range(PLANES - 1), 1)
     got_above = along(down, range(1, PLANES), -1)
+    got_across = permute(twice, lambda r: r ^ (2 * PLANE))
     sibling_a = permute(after(sent_a, mirror_3, *early), lambda r: r ^ 1)
     sibling_b = permute(after(sent_b, mirror_3, *early), lambda r: r ^ 1)
     other = permute(kept_b + sibling_b, lambda r: r ^ 2)
     *last, thrice = final(factors_a, factors_b, after(mirror_3, near_b))
-    got_mirror = mirrored(after(thrice, got_below, got_above, got_across))
+    got_mirror = mirrored(after(thrice, got_across, got_below, got_above))
     others = [
         permute(last[flip], functools.partial(lambda flip, r: r ^ flip, flip))
         for flip in range(1, PLANE)

time: 161 us -> 155 us (0.963)
  waiting for transfers between devices: 40.5 us -> 34.4 us
    ppermute x11, waiting for transfers between devices: 13.7 us -> 3.86 us  [permute(): return lax.ppermute(x, 'row', [(r, move(r)) for r in range(blocks)])]
    ppermute x8, waiting for transfers between devices: 26.7 us -> 30.5 us  [along(): lax.ppermute(x, 'row', [(p * PLANE + b, (p + step) * PLANE + b) for p in...]
    ppermute x11, starting transfers between devices: 20 us -> 16.8 us  [permute(): return lax.ppermute(x, 'row', [(r, move(r)) for r in range(blocks)])]
    ppermute x8, starting transfers between devices: 17.4 us -> 20.2 us  [along(): lax.ppermute(x, 'row', [(p * PLANE + b, (p + step) * PLANE + b) for p in...]
  transfers between devices with their start and end apart: 21 -> 21, of which waited for: 6 -> 7; matrix products, arithmetic and copies ran while one was open for 3% -> 3% of each run, Pallas kernels for 34% -> 35%
where the time goes in v3:
time: 155 us; the launch traced here: 154 us
  Pallas kernels  58.9 us (38%)
  starting transfers between devices  40.5 us (26%)
  waiting for transfers between devices  34.4 us (22%)
  local copies, waits for them, and re-layouts  15 us (10%)
  other arithmetic  3.26 us (2%)
  between operations  1.75 us (1%)
    pallas_call x3, Pallas kernels, product(): pl.pallas_call(functools.partial(product_kernel, t, flips, here, there, s...  32 us
    ppermute x8, waiting for transfers between devices, along(): lax.ppermute(x, 'row', [(p * PLANE + b, (p + step) * PLANE + b) for p in...  30.5 us
    ppermute x8, starting transfers between devices, along(): lax.ppermute(x, 'row', [(p * PLANE + b, (p + step) * PLANE + b) for p in...  20.2 us
    ppermute x11, starting transfers between devices, permute(): return lax.ppermute(x, 'row', [(r, move(r)) for r in range(blocks)])  16.8 us
    unnamed x42, local copies, waits for them, and re-layouts  12.9 us
    pallas_call x1, Pallas kernels, final(): pl.pallas_call(functools.partial(last_kernel, t, cap), grid=(PLANE,), out...  6.82 us
    pallas_call x1, Pallas kernels, spread(): pl.pallas_call(functools.partial(spread_kernel, t, flips, unroll), grid=(...  6.62 us
    pallas_call x1, Pallas kernels, planes_body(): pl.pallas_call(functools.partial(expand_kernel, t), out_shape=jax.ShapeDt...  5.05 us
  transfers between devices with their start and end apart: 21, of which 7 were waited for; matrix products, arithmetic and copies ran while one was open for 3% of the time, Pallas kernels for 35%

profile of v3, /device:TPU:1, one launch (start us, length us, event | category | flops | bytes accessed | tf_op | source)
XLA Modules:
  0.0 153.8 jit_solution(12843709143988046478)
XLA Ops:
  0.8 1.3 collective-permute-start.7
  2.0 5.3 %collective-permute-start.4 = (f32[128,2048]{1,0:T(8,128)}, f32[128,2048]{1,0:T(8,128)S(1)}, u32[]{:S(2)}, u32[]{:S(2)}) collective-permute-start(f32[128,2048]{1,0:T(8,128)} %refs_0_.5), channel_id=1, source_target_pairs={{0,4},{1,5},{2,6},{3,7},{4,8},{5,9},{6,10},{7,11},{8,12},{9,13},{1... | collective-permute-start | bytes 3145736 | tf_op jit(solution)/shard_map/ppermute | solution.py:353
  7.4 1.5 collective-permute-start.10
  8.9 0.9 reshape.21.s_ref
  9.7 0.9 fusion.1
  11.1 0.6 reduce_max.9
  12.7 0.7 concatenate.15.tab
  13.4 1.7 %copy-done.7 = f32[1,1024,512]{2,1,0:T(8,128)S(1)} copy-done((f32[1,1024,512]{2,1,0:T(8,128)S(1)}, f32[1,1024,512]{2,1,0:T(8,128)}, u32[]{:S(2)}) %copy-start.7) | copy-done | bytes 2097176
  15.1 6.6 %spread.1 = (bf16[2,2048,512]{2,1,0:T(8,128)(2,1)S(1)}, bf16[2,2048,512]{2,1,0:T(8,128)(2,1)S(1)}) custom-call(s32[530]{0:T(1024)S(1)} %concatenate.15.tab, s32[16,1,1024]{2,1,0:T(1,128)S(1)} %reshape.21.s_ref, f32[1,1024,512]{2,1,0:T(8,128)S(1)} %copy-done.7, f32[1,1024,512]{2,1,0:T(8,128)} %collective-permute-done.5.refs_1_), custom_call_target="tpu_custom_call" | custom-call | flops 268435456 | bytes 1572864 | tf_op jit(solution)/shard_map/spread/pallas_call | solution.py:367
  21.8 7.4 %collective-permute-done.7.refs_2_ = f32[128,2048]{1,0:T(8,128)S(1)} collective-permute-done((f32[128,2048]{1,0:T(8,128)}, f32[128,2048]{1,0:T(8,128)S(1)}, u32[]{:S(2)}, u32[]{:S(2)}) %collective-permute-start.7) | collective-permute-done | bytes 1048608 | tf_op jit(solution)/shard_map/ppermute | solution.py:353
  29.2 1.3 collective-permute-start.8
  30.5 0.7 collective-permute-start.6
  31.3 7.5 %product.3 = (f32[2,384,512]{2,1,0:T(8,128)S(1)}, f32[144,512]{1,0:T(8,128)S(1)}, f32[144,512]{1,0:T(8,128)S(1)}) custom-call(s32[530]{0:T(1024)S(1)} %concatenate.15.tab, s32[16,1,1024]{2,1,0:T(1,128)S(1)} %reshape.21.s_ref, f32[128,2048]{1,0:T(8,128)S(1)} %copy-done.6, f32[128,2048]{1,0:T(8,128)S(1)} %collective-permute-done.4.refs_1_, ...), custom_call_target="tpu_custom_call" | custom-call | flops 503316480 | bytes 1245184 | tf_op jit(solution)/shard_map/product/pallas_call | solution.py:388
  38.8 16.6 %collective-permute-done.8 = f32[128,2048]{1,0:T(8,128)S(1)} collective-permute-done((f32[128,2048]{1,0:T(8,128)S(1)}, f32[128,2048]{1,0:T(8,128)S(1)}, u32[]{:S(2)}, u32[]{:S(2)}) %collective-permute-start.8) | collective-permute-done | bytes 1048608 | tf_op jit(solution)/shard_map/ppermute | solution.py:353
  55.6 1.3 collective-permute-start.11
  56.9 1.3 collective-permute-start.9
  58.2 4.5 %collective-permute-start.16 = (f32[144,512]{1,0:T(8,128)S(1)}, f32[144,512]{1,0:T(8,128)S(1)}, u32[]{:S(2)}, u32[]{:S(2)}) collective-permute-start(f32[144,512]{1,0:T(8,128)S(1)} %get-tuple-element.83), channel_id=1, source_target_pairs={{0,4},{1,5},{2,6},{3,7},{4,8},{5,9},{6,10},{7,11},{8,12},{9,13},{1... | collective-permute-start | bytes 884744 | tf_op jit(solution)/shard_map/ppermute | solution.py:353
  62.7 1.5 collective-permute-start.17
  64.1 6.0 %product.4 = (f32[2,128,512]{2,1,0:T(8,128)}, f32[512,512]{1,0:T(8,128)S(1)}, f32[512,512]{1,0:T(8,128)S(1)}, f32[144,512]{1,0:T(8,128)S(1)}) custom-call(s32[530]{0:T(1024)S(1)} %concatenate.15.tab, s32[16,1,1024]{2,1,0:T(1,128)S(1)} %reshape.21.s_ref, f32[128,2048]{1,0:T(8,128)S(1)} %add.14.refs_0_.refs_3_, ...), custom_call_target="tpu_custom_call" | custom-call | flops 167772160 | bytes 1114112 | tf_op jit(solution)/shard_map/product/pallas_call | solution.py:388
  70.2 5.6 %collective-permute-start.18 = (f32[144,512]{1,0:T(8,128)S(1)}, f32[144,512]{1,0:T(8,128)S(1)}, u32[]{:S(2)}, u32[]{:S(2)}) collective-permute-start(f32[144,512]{1,0:T(8,128)S(1)} %get-tuple-element.85), channel_id=1, source_target_pairs={{0,8},{1,9},{2,10},{3,11},{4,12},{5,13},{6,14},{7,15},{8,0},{9,1},... | collective-permute-start | bytes 884744 | tf_op jit(solution)/shard_map/ppermute | solution.py:350
  75.7 18.4 %product.5 = (bf16[2,2048,512]{2,1,0:T(8,128)(2,1)S(1)}, bf16[2,2048,512]{2,1,0:T(8,128)(2,1)S(1)}, f32[2,512,512]{2,1,0:T(8,128)}, f32[512,512]{1,0:T(8,128)S(1...) custom-call(s32[530]{0:T(1024)S(1)} %concatenate.15.tab, ...), custom_call_target="tpu_custom_call" | custom-call | flops 671088640 | bytes 1310720 | tf_op jit(solution)/shard_map/product/pallas_call | solution.py:388
  94.2 2.6 %collective-permute-done.17.refs_1_ = f32[144,512]{1,0:T(8,128)S(1)} collective-permute-done((f32[144,512]{1,0:T(8,128)S(1)}, f32[144,512]{1,0:T(8,128)S(1)}, u32[]{:S(2)}, u32[]{:S(2)}) %collective-permute-start.17) | collective-permute-done | bytes 294944 | tf_op jit(solution)/shard_map/ppermute | solution.py:353
  96.8 0.7 collective-permute-start.20
  97.5 2.2 %collective-permute-done.20 = f32[512,512]{1,0:T(8,128)S(1)} collective-permute-done((f32[512,512]{1,0:T(8,128)S(1)}, f32[512,512]{1,0:T(8,128)S(1)}, u32[]{:S(2)}, u32[]{:S(2)}) %collective-permute-start.20) | collective-permute-done | bytes 1048608 | tf_op jit(solution)/shard_map/ppermute | solution.py:350
  99.8 1.2 add.15
  100.9 1.2 collective-permute-start.21
  102.2 2.8 %collective-permute-start.12 = (f32[144,512]{1,0:T(8,128)S(1)}, f32[144,512]{1,0:T(8,128)S(1)}, u32[]{:S(2)}, u32[]{:S(2)}) collective-permute-start(f32[144,512]{1,0:T(8,128)S(1)} %get-tuple-element.79), channel_id=1, source_target_pairs={{0,8},{1,9},{2,10},{3,11},{4,12},{5,13},{6,14},{7,15},{8,0},{9,1},... | collective-permute-start | bytes 884744 | tf_op jit(solution)/shard_map/ppermute | solution.py:350
  105.0 4.1 %collective-permute-start.13 = (f32[144,512]{1,0:T(8,128)S(1)}, f32[144,512]{1,0:T(8,128)S(1)}, u32[]{:S(2)}, u32[]{:S(2)}) collective-permute-start(f32[144,512]{1,0:T(8,128)S(1)} %get-tuple-element.80), channel_id=1, source_target_pairs={{0,4},{1,5},{2,6},{3,7},{4,8},{5,9},{6,10},{7,11},{8,12},{9,13},{1... | collective-permute-start | bytes 884744 | tf_op jit(solution)/shard_map/ppermute | solution.py:353
  109.1 1.5 collective-permute-start.14
  110.6 6.8 %last.1 = (f32[1,128,512]{2,1,0:T(8,128)}, f32[1,128,512]{2,1,0:T(8,128)}, f32[1,128,512]{2,1,0:T(8,128)}, f32[1,128,512]{2,1,0:T(8,128)}, f32[288,512]{1,0:T(8,128)}) custom-call(s32[530]{0:T(1024)S(1)} %concatenate.15.tab, s32[16,1,1024]{2,1,0:T(1,128)S(1)} %reshape.21.s_ref, f32[128,2048]{1,0:T(8,128)S(1)} %collective-permute-done.9.third_ref, ...), custom_call_target="tpu_custom_call" | custom-call | flops 335544320 | bytes 2097152 | tf_op jit(solution)/shard_map/last/pallas_call | solution.py:420
  118.1 0.7 copy-done.13
  118.8 0.7 copy-done.15
  119.5 3.8 %collective-permute-done.14.refs_4_ = f32[144,512]{1,0:T(8,128)S(1)} collective-permute-done((f32[144,512]{1,0:T(8,128)S(1)}, f32[144,512]{1,0:T(8,128)S(1)}, u32[]{:S(2)}, u32[]{:S(2)}) %collective-permute-start.14) | collective-permute-done | bytes 294944 | tf_op jit(solution)/shard_map/ppermute | solution.py:353
  123.3 0.7 copy-done.17
  124.0 2.2 %collective-permute-start.15 = (f32[288,512]{1,0:T(8,128)}, f32[288,512]{1,0:T(8,128)}, u32[]{:S(2)}, u32[]{:S(2)}) collective-permute-start(f32[288,512]{1,0:T(8,128)} %get-tuple-element.82), channel_id=1, source_target_pairs={{0,12},{1,13},{2,14},{3,15},{12,0},{13,1},{14,2},{15,3},{16,28},{1... | collective-permute-start | bytes 1769480 | tf_op jit(solution)/shard_map/ppermute | solution.py:359
  126.2 1.9 %collective-permute-start.22 = (f32[1,128,512]{2,1,0:T(8,128)}, f32[1,128,512]{2,1,0:T(8,128)}, u32[]{:S(2)}, u32[]{:S(2)}) collective-permute-start(f32[1,128,512]{2,1,0:T(8,128)} %get-tuple-element.92), channel_id=1, source_target_pairs={{0,1},{1,0},{2,3},{3,2},{4,5},{5,4},{6,7},{7,6},{8,9},{9,8},{10,11... | collective-permute-start | bytes 786440 | tf_op jit(solution)/shard_map/ppermute | solution.py:350
  128.3 1.5 collective-permute-start.24
  129.8 1.0 copy-done.10
  130.8 1.0 copy-done.12
  131.7 1.0 copy-done.14
  132.7 1.0 copy-done.16
  133.7 1.0 copy-done.18
  134.6 4.7 %unpack.1.lanes_in = f32[8192,128]{1,0:T(8,128)S(1)} custom-call(s32[530]{0:T(1024)S(1)} %concatenate.15.tab, s32[16,1,1024]{2,1,0:T(1,128)S(1)} %reshape.21.s_ref, f32[2,384,512]{2,1,0:T(8,128)} %copy-done.19, f32[2,512,512]{2,1,0:T(8,128)} %get-tuple-element.74.near_b, f32[144,512]{1,0:T(8,128)S(1)} %collective-permute-done.16.refs_0_, ...), custom_call_target="tpu_custom_call" | custom-call | flops 37748736 | bytes 354304 | tf_op jit(solution)/shard_map/unpack/pallas_call | solution.py:511
  139.4 2.0 %copy-done.4 = f32[8192,128]{1,0:T(8,128)} copy-done((f32[8192,128]{1,0:T(8,128)}, f32[8192,128]{1,0:T(8,128)S(1)}, u32[]{:S(2)}) %copy-start.4) | copy-done | bytes 4194328
  141.4 1.0 collective-permute-done.24.refs_3_
  142.4 3.7 %finish.1 = f32[1,512,512]{2,1,0:T(8,128)} custom-call(s32[530]{0:T(1024)S(1)} %concatenate.15.tab, f32[1,512,512]{2,1,0:T(8,128)S(1)} %copy-done.8, f32[512,512]{1,0:T(8,128)S(1)} %get-tuple-element.71.kept_ref, f32[512,512]{1,0:T(8,128)S(1)} %collective-permute-done.19.sibling_ref, f32[512,512]{1,0:T(8,128)S(1)} %collective-permute-done.21.other_ref, ...), custom_call_target="tpu_custom_call" | custom-call | flops 25165824 | bytes 491520 | tf_op jit(solution)/shard_map/finish/pallas_call | solution.py:446
  146.4 2.2 %copy-done.5 = f32[8192,128]{1,0:T(8,128)S(1)} copy-done((f32[8192,128]{1,0:T(8,128)S(1)}, f32[8192,128]{1,0:T(8,128)}, u32[]{:S(2)}) %copy-start.5) | copy-done | bytes 4194328
  148.5 5.1 %expand.1 = f32[2048,512]{1,0:T(8,128)} custom-call(s32[530]{0:T(1024)S(1)} %concatenate.15.tab, s32[16,1,1024]{2,1,0:T(1,128)S(1)} %reshape.21.s_ref, f32[288,512]{1,0:T(8,128)} %collective-permute-done.15.message, f32[8192,128]{1,0:T(8,128)S(1)} %copy-done.5, f32[4,224,512]{2,1,0:T(8,128)S(1)} %get-tuple-element.115.late_ref), custom_call_target="tpu_custom_call" | custom-call | flops 9437184 | bytes 524288 | tf_op jit(solution)/shard_map/expand/pallas_call | solution.py:553
  (60 shorter events, 2.5 us)
Async XLA Ops:
  0.6 12.8 %collective-permute-start.5 = (f32[1,1024,512]{2,1,0:T(8,128)}, f32[1,1024,512]{2,1,0:T(8,128)}, u32[]{:S(2)}, u32[]{:S(2)}) collective-permute-start(f32[1,1024,512]{2,1,0:T(8,128)} %refs_0_.3), channel_id=1, source_target_pairs={{0,1},{1,0},{2,3},{3,2},{4,5},{5,4},{6,7},{7,6},{8,9},{9,8},{10,11... | collective-permute-start | bytes 6291464 | tf_op jit(solution)/shard_map/ppermute | solution.py:350
  0.8 28.5 %collective-permute-start.7 = (f32[128,2048]{1,0:T(8,128)}, f32[128,2048]{1,0:T(8,128)S(1)}, u32[]{:S(2)}, u32[]{:S(2)}) collective-permute-start(f32[128,2048]{1,0:T(8,128)} %refs_0_.5), channel_id=1, source_target_pairs={{4,0},{5,1},{6,2},{7,3},{8,4},{9,5},{10,6},{11,7},{12,8},{13,9},{1... | collective-permute-start | bytes 3145736 | tf_op jit(solution)/shard_map/ppermute | solution.py:353
  2.0 28.5 %collective-permute-start.4 = (f32[128,2048]{1,0:T(8,128)}, f32[128,2048]{1,0:T(8,128)S(1)}, u32[]{:S(2)}, u32[]{:S(2)}) collective-permute-start(f32[128,2048]{1,0:T(8,128)} %refs_0_.5), channel_id=1, source_target_pairs={{0,4},{1,5},{2,6},{3,7},{4,8},{5,9},{6,10},{7,11},{8,12},{9,13},{1... | collective-permute-start | bytes 3145736 | tf_op jit(solution)/shard_map/ppermute | solution.py:353
  7.4 48.2 %collective-permute-start.10 = (f32[1,1024,512]{2,1,0:T(8,128)}, f32[1,1024,512]{2,1,0:T(8,128)}, u32[]{:S(2)}, u32[]{:S(2)}) collective-permute-start(f32[1,1024,512]{2,1,0:T(8,128)} %refs_0_.3), channel_id=1, source_target_pairs={{0,2},{1,3},{2,0},{3,1},{4,6},{5,7},{6,4},{7,5},{8,10},{9,11},{10,... | collective-permute-start | bytes 6291464 | tf_op jit(solution)/shard_map/ppermute | solution.py:350
  13.4 17.8 %copy-start.6 = (f32[128,2048]{1,0:T(8,128)S(1)}, f32[128,2048]{1,0:T(8,128)}, u32[]{:S(2)}) copy-start(f32[128,2048]{1,0:T(8,128)} %refs_0_.5) | copy-start | bytes 3145732
  13.4 1.7 %copy-start.7 = (f32[1,1024,512]{2,1,0:T(8,128)S(1)}, f32[1,1024,512]{2,1,0:T(8,128)}, u32[]{:S(2)}) copy-start(f32[1,1024,512]{2,1,0:T(8,128)} %refs_0_.3) | copy-start | bytes 6291460
  21.8 88.8 %copy-start = (bf16[2,2048,512]{2,1,0:T(8,128)(2,1)}, bf16[2,2048,512]{2,1,0:T(8,128)(2,1)S(1)}, u32[]{:S(2)}) copy-start(bf16[2,2048,512]{2,1,0:T(8,128)(2,1)S(1)} %get-tuple-element.65.refs_3_.refs_2_.hi_a.refs_4_.refs_5_.refs_6_.refs_7_) | copy-start | bytes 12582916
  21.8 88.8 %copy-start.2 = (bf16[2,2048,512]{2,1,0:T(8,128)(2,1)}, bf16[2,2048,512]{2,1,0:T(8,128)(2,1)S(1)}, u32[]{:S(2)}) copy-start(bf16[2,2048,512]{2,1,0:T(8,128)(2,1)S(1)} %get-tuple-element.66.refs_4_.refs_3_.lo_a.refs_8_.refs_9_.refs_10_.refs_11_) | copy-start | bytes 12582916
  29.2 26.2 %collective-permute-start.8 = (f32[128,2048]{1,0:T(8,128)S(1)}, f32[128,2048]{1,0:T(8,128)S(1)}, u32[]{:S(2)}, u32[]{:S(2)}) collective-permute-start(f32[128,2048]{1,0:T(8,128)S(1)} %collective-permute-done.7.refs_2_), channel_id=1, source_target_pairs={{4,0},{5,1},{6,2},{7,3},{8,4},{9,5},{10,6},{11,7},{20,16},{21,17},... | collective-permute-start | bytes 3145736 | tf_op jit(solution)/shard_map/ppermute | solution.py:353
  30.5 24.9 %collective-permute-start.6 = (f32[128,2048]{1,0:T(8,128)S(1)}, f32[128,2048]{1,0:T(8,128)S(1)}, u32[]{:S(2)}, u32[]{:S(2)}) collective-permute-start(f32[128,2048]{1,0:T(8,128)S(1)} %collective-permute-done.4.refs_1_), channel_id=1, source_target_pairs={{4,8},{5,9},{6,10},{7,11},{8,12},{9,13},{10,14},{11,15},{20,24},{2... | collective-permute-start | bytes 3145736 | tf_op jit(solution)/shard_map/ppermute | solution.py:353
  38.8 31.4 %copy-start.19 = (f32[2,384,512]{2,1,0:T(8,128)}, f32[2,384,512]{2,1,0:T(8,128)S(1)}, u32[]{:S(2)}) copy-start(f32[2,384,512]{2,1,0:T(8,128)S(1)} %get-tuple-element.96.refs_1_.near_a) | copy-start | bytes 4718596
  55.6 20.2 %collective-permute-start.11 = (f32[1,1024,512]{2,1,0:T(8,128)}, f32[1,1024,512]{2,1,0:T(8,128)S(1)}, u32[]{:S(2)}, u32[]{:S(2)}) collective-permute-start(f32[1,1024,512]{2,1,0:T(8,128)} %collective-permute-done.10.refs_4_), channel_id=1, source_target_pairs={{0,1},{1,0},{2,3},{3,2},{4,5},{5,4},{6,7},{7,6},{8,9},{9,8},{10,11... | collective-permute-start | bytes 6291464 | tf_op jit(solution)/shard_map/ppermute | solution.py:350
  56.9 39.9 %collective-permute-start.9 = (f32[128,2048]{1,0:T(8,128)S(1)}, f32[128,2048]{1,0:T(8,128)S(1)}, u32[]{:S(2)}, u32[]{:S(2)}) collective-permute-start(f32[128,2048]{1,0:T(8,128)S(1)} %add.14.refs_0_.refs_3_), channel_id=1, source_target_pairs={{4,0},{5,1},{6,2},{7,3},{8,12},{9,13},{10,14},{11,15},{20,16},{21,... | collective-permute-start | bytes 3145736 | tf_op jit(solution)/shard_map/ppermute | solution.py:478
  58.2 36.0 %collective-permute-start.16 = (f32[144,512]{1,0:T(8,128)S(1)}, f32[144,512]{1,0:T(8,128)S(1)}, u32[]{:S(2)}, u32[]{:S(2)}) collective-permute-start(f32[144,512]{1,0:T(8,128)S(1)} %get-tuple-element.83), channel_id=1, source_target_pairs={{0,4},{1,5},{2,6},{3,7},{4,8},{5,9},{6,10},{7,11},{8,12},{9,13},{1... | collective-permute-start | bytes 884744 | tf_op jit(solution)/shard_map/ppermute | solution.py:353
  62.7 34.1 %collective-permute-start.17 = (f32[144,512]{1,0:T(8,128)S(1)}, f32[144,512]{1,0:T(8,128)S(1)}, u32[]{:S(2)}, u32[]{:S(2)}) collective-permute-start(f32[144,512]{1,0:T(8,128)S(1)} %get-tuple-element.84), channel_id=1, source_target_pairs={{4,0},{5,1},{6,2},{7,3},{8,4},{9,5},{10,6},{11,7},{12,8},{13,9},{1... | collective-permute-start | bytes 884744 | tf_op jit(solution)/shard_map/ppermute | solution.py:353
  70.2 26.6 %collective-permute-start.18 = (f32[144,512]{1,0:T(8,128)S(1)}, f32[144,512]{1,0:T(8,128)S(1)}, u32[]{:S(2)}, u32[]{:S(2)}) collective-permute-start(f32[144,512]{1,0:T(8,128)S(1)} %get-tuple-element.85), channel_id=1, source_target_pairs={{0,8},{1,9},{2,10},{3,11},{4,12},{5,13},{6,14},{7,15},{8,0},{9,1},... | collective-permute-start | bytes 884744 | tf_op jit(solution)/shard_map/ppermute | solution.py:350
  96.8 20.6 %copy-start.9 = (f32[144,512]{1,0:T(8,128)}, f32[144,512]{1,0:T(8,128)S(1)}, u32[]{:S(2)}) copy-start(f32[144,512]{1,0:T(8,128)S(1)} %collective-permute-done.17.refs_1_) | copy-start | bytes 884740
  96.8 20.6 %copy-start.11 = (f32[144,512]{1,0:T(8,128)}, f32[144,512]{1,0:T(8,128)S(1)}, u32[]{:S(2)}) copy-start(f32[144,512]{1,0:T(8,128)S(1)} %collective-permute-done.18.refs_2_) | copy-start | bytes 884740
  96.8 3.0 %collective-permute-start.20 = (f32[512,512]{1,0:T(8,128)S(1)}, f32[512,512]{1,0:T(8,128)S(1)}, u32[]{:S(2)}, u32[]{:S(2)}) collective-permute-start(f32[512,512]{1,0:T(8,128)S(1)} %get-tuple-element.90), channel_id=1, source_target_pairs={{0,1},{1,0},{2,3},{3,2},{4,5},{5,4},{6,7},{7,6},{8,9},{9,8},{10,11... | collective-permute-start | bytes 3145736 | tf_op jit(solution)/shard_map/ppermute | solution.py:350
  97.5 30.9 %collective-permute-start.19 = (f32[512,512]{1,0:T(8,128)S(1)}, f32[512,512]{1,0:T(8,128)S(1)}, u32[]{:S(2)}, u32[]{:S(2)}) collective-permute-start(f32[512,512]{1,0:T(8,128)S(1)} %get-tuple-element.87), channel_id=1, source_target_pairs={{0,1},{1,0},{2,3},{3,2},{4,5},{5,4},{6,7},{7,6},{8,9},{9,8},{10,11... | collective-permute-start | bytes 3145736 | tf_op jit(solution)/shard_map/ppermute | solution.py:350
  100.9 41.4 %collective-permute-start.21 = (f32[512,512]{1,0:T(8,128)}, f32[512,512]{1,0:T(8,128)S(1)}, u32[]{:S(2)}, u32[]{:S(2)}) collective-permute-start(f32[512,512]{1,0:T(8,128)} %add.15), channel_id=1, source_target_pairs={{0,2},{1,3},{2,0},{3,1},{4,6},{5,7},{6,4},{7,5},{8,10},{9,11},{10,... | collective-permute-start | bytes 3145736 | tf_op jit(solution)/shard_map/ppermute | solution.py:350
  102.2 15.9 %collective-permute-start.12 = (f32[144,512]{1,0:T(8,128)S(1)}, f32[144,512]{1,0:T(8,128)S(1)}, u32[]{:S(2)}, u32[]{:S(2)}) collective-permute-start(f32[144,512]{1,0:T(8,128)S(1)} %get-tuple-element.79), channel_id=1, source_target_pairs={{0,8},{1,9},{2,10},{3,11},{4,12},{5,13},{6,14},{7,15},{8,0},{9,1},... | collective-permute-start | bytes 884744 | tf_op jit(solution)/shard_map/ppermute | solution.py:350
  105.0 13.8 %collective-permute-start.13 = (f32[144,512]{1,0:T(8,128)S(1)}, f32[144,512]{1,0:T(8,128)S(1)}, u32[]{:S(2)}, u32[]{:S(2)}) collective-permute-start(f32[144,512]{1,0:T(8,128)S(1)} %get-tuple-element.80), channel_id=1, source_target_pairs={{0,4},{1,5},{2,6},{3,7},{4,8},{5,9},{6,10},{7,11},{8,12},{9,13},{1... | collective-permute-start | bytes 884744 | tf_op jit(solution)/shard_map/ppermute | solution.py:353
  109.1 14.2 %collective-permute-start.14 = (f32[144,512]{1,0:T(8,128)S(1)}, f32[144,512]{1,0:T(8,128)S(1)}, u32[]{:S(2)}, u32[]{:S(2)}) collective-permute-start(f32[144,512]{1,0:T(8,128)S(1)} %get-tuple-element.81), channel_id=1, source_target_pairs={{4,0},{5,1},{6,2},{7,3},{8,4},{9,5},{10,6},{11,7},{12,8},{13,9},{1... | collective-permute-start | bytes 884744 | tf_op jit(solution)/shard_map/ppermute | solution.py:353
  118.1 0.7 copy-start.13
  118.8 0.7 copy-start.15
  123.3 0.7 copy-start.17
  124.0 22.1 %collective-permute-start.15 = (f32[288,512]{1,0:T(8,128)}, f32[288,512]{1,0:T(8,128)}, u32[]{:S(2)}, u32[]{:S(2)}) collective-permute-start(f32[288,512]{1,0:T(8,128)} %get-tuple-element.82), channel_id=1, source_target_pairs={{0,12},{1,13},{2,14},{3,15},{12,0},{13,1},{14,2},{15,3},{16,28},{1... | collective-permute-start | bytes 1769480 | tf_op jit(solution)/shard_map/ppermute | solution.py:359
  126.2 15.1 %collective-permute-start.22 = (f32[1,128,512]{2,1,0:T(8,128)}, f32[1,128,512]{2,1,0:T(8,128)}, u32[]{:S(2)}, u32[]{:S(2)}) collective-permute-start(f32[1,128,512]{2,1,0:T(8,128)} %get-tuple-element.92), channel_id=1, source_target_pairs={{0,1},{1,0},{2,3},{3,2},{4,5},{5,4},{6,7},{7,6},{8,9},{9,8},{10,11... | collective-permute-start | bytes 786440 | tf_op jit(solution)/shard_map/ppermute | solution.py:350
  128.1 13.3 %collective-permute-start.23 = (f32[1,128,512]{2,1,0:T(8,128)}, f32[1,128,512]{2,1,0:T(8,128)}, u32[]{:S(2)}, u32[]{:S(2)}) collective-permute-start(f32[1,128,512]{2,1,0:T(8,128)} %get-tuple-element.93), channel_id=1, source_target_pairs={{0,2},{1,3},{2,0},{3,1},{4,6},{5,7},{6,4},{7,5},{8,10},{9,11},{10,... | collective-permute-start | bytes 786440 | tf_op jit(solution)/shard_map/ppermute | solution.py:350
  128.3 14.0 %collective-permute-start.24 = (f32[1,128,512]{2,1,0:T(8,128)}, f32[1,128,512]{2,1,0:T(8,128)}, u32[]{:S(2)}, u32[]{:S(2)}) collective-permute-start(f32[1,128,512]{2,1,0:T(8,128)} %get-tuple-element.94), channel_id=1, source_target_pairs={{0,3},{1,2},{2,1},{3,0},{4,7},{5,6},{6,5},{7,4},{8,11},{9,10},{10,... | collective-permute-start | bytes 786440 | tf_op jit(solution)/shard_map/ppermute | solution.py:350
  129.8 1.0 copy-start.10
  130.8 1.0 copy-start.12
  131.7 1.0 copy-start.14
  132.7 1.0 copy-start.16
  133.7 1.0 copy-start.18
  134.6 7.8 %copy-start.1 = (bf16[2,2048,512]{2,1,0:T(8,128)(2,1)S(1)}, bf16[2,2048,512]{2,1,0:T(8,128)(2,1)}, u32[]{:S(2)}) copy-start(bf16[2,2048,512]{2,1,0:T(8,128)(2,1)} %copy-done) | copy-start | bytes 12582916
  134.6 7.8 %copy-start.3 = (bf16[2,2048,512]{2,1,0:T(8,128)(2,1)S(1)}, bf16[2,2048,512]{2,1,0:T(8,128)(2,1)}, u32[]{:S(2)}) copy-start(bf16[2,2048,512]{2,1,0:T(8,128)(2,1)} %copy-done.2) | copy-start | bytes 12582916
  134.6 7.8 %copy-start.8 = (f32[1,512,512]{2,1,0:T(8,128)S(1)}, f32[1,512,512]{2,1,0:T(8,128)}, u32[]{:S(2)}) copy-start(f32[1,512,512]{2,1,0:T(8,128)} %diag_ref.1) | copy-start | bytes 3145732
  134.6 7.8 %copy-start.21 = (f32[1,128,512]{2,1,0:T(8,128)S(1)}, f32[1,128,512]{2,1,0:T(8,128)}, u32[]{:S(2)}) copy-start(f32[1,128,512]{2,1,0:T(8,128)} %get-tuple-element.91.refs_0_) | copy-start | bytes 786436
  139.4 2.0 %copy-start.4 = (f32[8192,128]{1,0:T(8,128)}, f32[8192,128]{1,0:T(8,128)S(1)}, u32[]{:S(2)}) copy-start(f32[8192,128]{1,0:T(8,128)S(1)} %unpack.1.lanes_in) | copy-start | bytes 12582916
  146.4 2.2 %copy-start.5 = (f32[8192,128]{1,0:T(8,128)S(1)}, f32[8192,128]{1,0:T(8,128)}, u32[]{:S(2)}) copy-start(f32[8192,128]{1,0:T(8,128)} %copy-done.4) | copy-start | bytes 12582916
